TPU v7x, 32 devices: a whole 2x2x4 slice. The times are simulated.
32 devices in a mesh: gx: 4 (over y, x), gy: 8 (over z, core).
Axes of the slice: x: 2, y: 2, z: 4, core: 2. Of those that a mesh axis runs over, the one named last changes fastest.
Arguments:
- scalar_field: float32 [64, 256, 1024], P(None, 'gy', 'gx'), may hold values from -6 to 6
- velocity: bfloat16 [3, 64, 256, 1024], P(None, None, 'gy', 'gx'), may hold values from -4 to 4
- shear_offset: int32 [2], replicated, may hold values from 0 to 1023
- part_temp: float32 [32, 32, 64], P(('gx', 'gy')), may hold values from -6 to 6
- part_coef: float32 [32, 32, 64], P(('gx', 'gy')), may hold values from 0.5 to 4
- part_heat: float32 [32, 32, 64], P(('gx', 'gy')), may hold values from 0.2 to 2
- part_cell: int32 [32, 32, 64], P(('gx', 'gy')), may hold values from 0 to 524287
- part_count: int32 [32, 32], P(('gx', 'gy')), may hold values from 0 to 64, as said below
Outputs:
- scalar_out: float32 [64, 256, 1024], P(None, 'gy', 'gx')
- temp_out: float32 [32, 32, 64], P(('gx', 'gy'))
Inputs may be any that keep to these rules, and one draw needn't show every extreme that they name: Slots below part_count[s, d] are live; in every draw one owning device receives 64 live slots from every holding device, and another receives none.
All inputs are finite; a program needn't handle non-finite values.
Results may differ from a plain program's by a relative error of at most 0.0003.
Values sent between devices are 32-bit elements; how exact they have to be, the bound alone decides.
A program may use at most 64 MiB of HBM per device.

v0:
```python
import jax
import jax.numpy as jnp
from jax import lax
from jax.sharding import PartitionSpec as P

CX = 256
CY = 32
NZ = 64
CAP = 64


time_step = 0.1
diffusivity = 0.1
mean_speed = 1.0
mean_gradient = 1.0
heat_share = 0.5


def padded(shard, sides, width):
    for axis, dim in sides:
        count, length = (lax.axis_size(axis), shard.shape[dim])
        up = [(i, (i + 1) % count) for i in range(count)]
        down = [(j, i) for i, j in up]
        last = lax.slice_in_dim(shard, length - width, length, axis=dim)
        leading = lax.slice_in_dim(shard, 0, width, axis=dim)
        before = lax.ppermute(last, axis, up)
        after = lax.ppermute(leading, axis, down)
        shard = jnp.concatenate([before, shard, after], axis=dim)
    return shard


def derivative(extended, axis, length):
    minus_two = lax.slice_in_dim(extended, 0, length, axis=axis)
    minus_one = lax.slice_in_dim(extended, 1, length + 1, axis=axis)
    center = lax.slice_in_dim(extended, 2, length + 2, axis=axis)
    plus_one = lax.slice_in_dim(extended, 3, length + 3, axis=axis)
    plus_two = lax.slice_in_dim(extended, 4, length + 4, axis=axis)
    grad = (8.0 * (plus_one - minus_one) - (plus_two - minus_two)) / 12.0
    lap = (16.0 * (plus_one + minus_one) - (plus_two + minus_two) - 30.0 * center) / 12.0
    return (grad, lap)


def tendency(center, x_extended, y_extended, z_extended, velocity, mean_flow, source):
    grad_x, lap_x = derivative(x_extended, 2, center.shape[2])
    grad_y, lap_y = derivative(y_extended, 1, center.shape[1])
    grad_z, lap_z = derivative(z_extended, 0, center.shape[0])
    along_x = velocity[0].astype(jnp.float32)
    along_y = velocity[1].astype(jnp.float32)
    along_z = velocity[2].astype(jnp.float32)
    return (
        -(along_x + mean_flow) * grad_x
        - along_y * grad_y
        - along_z * grad_z
        - mean_gradient * along_y
        + diffusivity * (lap_x + lap_y + lap_z)
        + heat_share * source
    )


def shear_move(ghosts, shifts, gx_index, full_x):
    gathered = lax.all_gather(ghosts, "gx", axis=3, tiled=True)
    doubled = jnp.concatenate([gathered, gathered], axis=3)
    pieces = []
    for slab in range(2):
        start = (gx_index * CX - shifts[slab]) % full_x
        pieces.append(lax.dynamic_slice_in_dim(doubled[slab], start, CX, 2))
    return jnp.stack(pieces)


def cell_list(part_cell):
    return lax.all_to_all(part_cell, ("gx", "gy"), split_axis=1, concat_axis=0, tiled=True)


def flux_home(flux):
    return lax.all_to_all(flux, ("gx", "gy"), split_axis=0, concat_axis=1, tiled=True)


def on_device(
    scalar_field, velocity, shear_offset, part_temp, part_coef, part_heat, part_cell, part_count
):
    gx_index = lax.axis_index("gx")
    gy_index = lax.axis_index("gy")
    gy_count = lax.axis_size("gy")
    full_x = CX * lax.axis_size("gx")
    full_y = CY * gy_count
    rows_y = (gy_index * CY + jnp.arange(CY)).astype(jnp.float32)
    mean_flow = (mean_speed * (2.0 * (rows_y + 0.5) / full_y - 1.0))[:, None]
    slots = jnp.arange(CAP)
    live_slot = slots[None, None, :] < part_count[:, :, None]
    live_coef = jnp.where(live_slot, part_coef, jnp.float32(0.0))

    def sample_at(field, cells):
        return field.reshape(-1)[cells]

    def field_rhs(field, offset, flux, cells):
        source = (
            jnp.zeros(NZ * CY * CX, jnp.float32)
            .at[cells.reshape(-1)]
            .add(flux.reshape(-1))
            .reshape(NZ, CY, CX)
        )
        x_extended = padded(field, (("gx", 2),), 2)
        y_raw = padded(field, (("gy", 1),), 2)
        ghosts = jnp.stack([y_raw[:, :2], y_raw[:, -2:]])
        low_shift = jnp.where(gy_index == 0, (full_x - offset) % full_x, 0)
        high_shift = jnp.where(gy_index == gy_count - 1, offset, 0)
        moved = shear_move(ghosts, jnp.stack([low_shift, high_shift]), gx_index, full_x)
        y_extended = jnp.concatenate([moved[0], field, moved[1]], axis=1)
        z_extended = jnp.concatenate([field[-2:], field, field[:2]], axis=0)
        return tendency(field, x_extended, y_extended, z_extended, velocity, mean_flow, source)

    cells = cell_list(part_cell)
    arrived_temp, owned_coef = (
        lax.all_to_all(part_temp, ("gx", "gy"), split_axis=1, concat_axis=0, tiled=True),
        lax.all_to_all(live_coef, ("gx", "gy"), split_axis=1, concat_axis=0, tiled=True),
    )
    flux_one = owned_coef * (arrived_temp - sample_at(scalar_field, cells))
    back_one = flux_home(flux_one)
    section_one = scalar_field + time_step * field_rhs(
        scalar_field, shear_offset[0], flux_one, cells
    )
    temp_one = part_temp + time_step * (part_heat - back_one)
    arrived_two = lax.all_to_all(temp_one, ("gx", "gy"), split_axis=1, concat_axis=0, tiled=True)
    flux_two = owned_coef * (arrived_two - sample_at(section_one, cells))
    back_two = flux_home(flux_two)
    scalar_out = 0.75 * scalar_field + 0.25 * (
        section_one + time_step * field_rhs(section_one, shear_offset[1], flux_two, cells)
    )
    temp_two = 0.75 * part_temp + 0.25 * (temp_one + time_step * (part_heat - back_two))
    temp_out = jnp.where(live_slot, temp_two, jnp.float32(0.0))
    return (scalar_out, temp_out)


def solution(mesh):
    in_specs = (
        P(None, "gy", "gx"),
        P(None, None, "gy", "gx"),
        P(),
        P(("gx", "gy"), None, None),
        P(("gx", "gy"), None, None),
        P(("gx", "gy"), None, None),
        P(("gx", "gy"), None, None),
        P(("gx", "gy"), None),
    )
    out_specs = (P(None, "gy", "gx"), P(("gx", "gy"), None, None))
    return jax.shard_map(
        on_device, mesh=mesh, in_specs=in_specs, out_specs=out_specs, check_vma=False
    )
```

profile of v0, /device:TPU:0, one launch (start us, length us, event | category | flops | bytes accessed | tf_op | source)
XLA Modules:
  0.0 206.8 jit_solution(8684981412774948687)
XLA Ops:
  9.0 4.1 %collective-permute-start.3 = (f32[64,2,256]{2,1,0:T(2,128)S(1)}, f32[64,2,256]{2,1,0:T(2,128)S(1)}, u32[]{:S(2)}, u32[]{:S(2)}) collective-permute-start(f32[64,2,256]{2,1,0:T(2,128)S(1)} %get-tuple-element.19), channel_id=1, source_target_pairs={{1,0},{2,1},{3,2},{4,3},{5,4},{6,5},{7,6},{0,7},{9,8},{10,9},{11,1... | collective-permute-start | bytes 393224 | tf_op jit(solution)/shard_map/ppermute | solution.py:27
  13.1 4.5 %all-to-all-start = ((s32[1,32,64]{2,0,1:T(1,128)}), s32[1,32,64]{2,0,1:T(1,128)S(1)}, u32[]{:S(2)}, u32[]{:S(2)}) async-start(s32[1,32,64]{2,0,1:T(1,128)} %bitcast.101), calls=%async_computation | async-start | bytes 32768 | tf_op jit(solution)/shard_map/all_to_all | solution.py:71
  17.6 1.9 fusion.47
  20.2 2.7 %collective-permute-start = (f32[64,32,2]{0,1,2:T(8,128)S(1)}, f32[64,32,2]{0,1,2:T(8,128)S(1)}, u32[]{:S(2)}, u32[]{:S(2)}) collective-permute-start(f32[64,32,2]{0,1,2:T(8,128)S(1)} %copy.73), channel_id=1, source_target_pairs={{8,0},{16,8},{24,16},{0,24},{9,1},{17,9},{25,17},{1,25},{10,2},{18... | collective-permute-start | bytes 49160 | tf_op jit(solution)/shard_map/ppermute | solution.py:27
  28.2 2.7 %copy.75 = f32[256,2,8,128]{3,1,2,0:T(2,128)S(1)} copy(f32[256,2,8,128]{3,2,1,0:T(8,128)} %bitcast.87) | data formatting | bytes 4194304
  30.9 6.1 %all-to-all-start.1 = ((f32[1,32,64]{2,0,1:T(1,128)}), f32[1,32,64]{2,0,1:T(1,128)S(1)}, u32[]{:S(2)}, u32[]{:S(2)}) async-start(f32[1,32,64]{2,0,1:T(1,128)} %bitcast.11), calls=%async_computation.1 | async-start | bytes 32768 | tf_op jit(solution)/shard_map/all_to_all | solution.py:115
  37.1 7.0 %all-to-all-done.1 = f32[1,32,64]{2,0,1:T(1,128)S(1)} async-done(((f32[1,32,64]{2,0,1:T(1,128)}), f32[1,32,64]{2,0,1:T(1,128)S(1)}, u32[]{:S(2)}, u32[]{:S(2)}) %all-to-all-start.1) | async-done | bytes 8224 | tf_op jit(solution)/shard_map/all_to_all | solution.py:115
  44.1 2.5 %all-to-all-start.2 = ((f32[1,32,64]{2,0,1:T(1,128)}), f32[1,32,64]{2,0,1:T(1,128)S(1)}, u32[]{:S(2)}, u32[]{:S(2)}) async-start(f32[1,32,64]{2,0,1:T(1,128)} %bitcast.12), calls=%async_computation.2 | async-start | bytes 32768 | tf_op jit(solution)/shard_map/all_to_all | solution.py:114
  48.0 5.7 %all-to-all-done.2 = f32[1,32,64]{2,0,1:T(1,128)S(1)} async-done(((f32[1,32,64]{2,0,1:T(1,128)}), f32[1,32,64]{2,0,1:T(1,128)S(1)}, u32[]{:S(2)}, u32[]{:S(2)}) %all-to-all-start.2) | async-done | bytes 8224 | tf_op jit(solution)/shard_map/all_to_all | solution.py:114
  55.8 11.8 %gather_fusion = f32[2048]{0:T(1024)S(1)} fusion(f32[524288]{0:T(1024)S(1)} %bitcast.85, s32[2048]{0:T(1024)S(1)} %broadcast_clamp_fusion), kind=kCustom, calls=%fused_computation | custom fusion | bytes 24576 | tf_op jit(solution)/shard_map/gather | solution.py:93
  68.3 2.5 %all-to-all-start.3 = ((f32[32,1,64]{2,1,0:T(1,128)}), f32[32,1,64]{2,1,0:T(1,128)S(1)}, u32[]{:S(2)}, u32[]{:S(2)}) async-start(f32[32,1,64]{2,1,0:T(1,128)} %bitcast.23), calls=%async_computation.3 | async-start | bytes 32768 | tf_op jit(solution)/shard_map/all_to_all | solution.py:75
  70.9 11.8 %scatter_custom_fusion = f32[524288]{0:T(1024)S(1)} fusion(s32[2048]{0:T(1024)S(1)} %bitcast.102, f32[2048]{0:T(1024)S(1)} %subtract_multiply_fusion.1, f32[]{:T(128)} %constant.99.clone.1), kind=kCustom, calls=%fused_computation.82 | custom fusion | flops 2048 | bytes 2097156 | tf_op jit(solution)/shard_map/scatter-add | solution.py:99
  84.0 5.8 %all-to-all-start.4 = ((f32[1,32,64]{2,0,1:T(1,128)}), f32[1,32,64]{2,0,1:T(1,128)S(1)}, u32[]{:S(2)}, u32[]{:S(2)}) async-start(f32[1,32,64]{2,0,1:T(1,128)} %bitcast.25), calls=%async_computation.4 | async-start | bytes 32768 | tf_op jit(solution)/shard_map/all_to_all | solution.py:123
  92.3 1.9 mul.175
  95.1 1.8 copy.62
  97.8 22.5 %all-gather.3.cloned.1.call-done = f32[2,64,2,1024]{3,2,1,0:T(2,128)} async-done(((f32[2,64,2,256]{3,2,1,0:T(2,128)}), f32[2,64,2,1024]{3,2,1,0:T(2,128)}) %all-gather.3.cloned.1.call-update) | async-done | bytes 1048592 | tf_op jit(solution)/shard_map/all_gather | solution.py:61
  120.2 1.5 constant_dynamic-update-slice_fusion.1
  124.6 6.7 %fusion.18 = f32[64,32,256]{2,1,0:T(8,128)S(1)} fusion(f32[64,32,256]{2,1,0:T(8,128)S(1)} %copy-done, f32[64,32,256]{2,1,0:T(8,128)S(1)} %mul.175, f32[2,32,256]{2,1,0:T(8,128)S(1)} %get-tuple-element.21, f32[2,32,256]{2,1,0:T(8,128)S(1)} %get-tuple-element.20, f32[64,2,256]{2,1,0:T(2,128)S(1)} %get-tuple-element.25, ...), kind=kLoop, calls=%fused_computation.52 | loop fusion | flops 31981568 | bytes 9863296 | tf_op jit(solution)/shard_map/add | solution.py:119
  131.5 3.5 %collective-permute-start.7 = (f32[64,2,256]{2,1,0:T(2,128)S(1)}, f32[64,2,256]{2,1,0:T(2,128)S(1)}, u32[]{:S(2)}, u32[]{:S(2)}) collective-permute-start(f32[64,2,256]{2,1,0:T(2,128)S(1)} %get-tuple-element.11), channel_id=1, source_target_pairs={{1,0},{2,1},{3,2},{4,3},{5,4},{6,5},{7,6},{0,7},{9,8},{10,9},{11,1... | collective-permute-start | bytes 393224 | tf_op jit(solution)/shard_map/ppermute | solution.py:27
  136.1 11.8 %gather_fusion.1 = f32[2048]{0:T(1024)S(1)} fusion(f32[524288]{0:T(1024)S(1)} %bitcast.86, s32[2048]{0:T(1024)S(1)} %broadcast_clamp_fusion), kind=kCustom, calls=%fused_computation.1 | custom fusion | bytes 24576 | tf_op jit(solution)/shard_map/gather | solution.py:93
  147.9 12.7 %scatter_custom_fusion.1 = f32[524288]{0:T(1024)} fusion(s32[2048]{0:T(1024)S(1)} %bitcast.103, f32[2048]{0:T(1024)S(1)} %subtract_multiply_fusion, f32[]{:T(128)} %constant.99.clone.1), kind=kCustom, calls=%fused_computation.80 | custom fusion | flops 2048 | bytes 2097156 | tf_op jit(solution)/shard_map/scatter-add | solution.py:99
  161.5 3.2 %broadcast_multiply_fusion = f32[524288]{0:T(1024)} fusion(f32[524288]{0:T(1024)} %scatter_custom_fusion.1), kind=kLoop, calls=%fused_computation.78 | loop fusion | flops 524288 | bytes 4194304 | tf_op jit(solution)/shard_map/mul | solution.py:56
  165.4 2.8 %all-to-all-start.5 = ((f32[32,1,64]{2,1,0:T(1,128)}), f32[32,1,64]{2,1,0:T(1,128)S(1)}, u32[]{:S(2)}, u32[]{:S(2)}) async-start(f32[32,1,64]{2,1,0:T(1,128)} %bitcast.27), calls=%async_computation.5 | async-start | bytes 32768 | tf_op jit(solution)/shard_map/all_to_all | solution.py:75
  169.6 2.9 %mul.192 = f32[64,32,256]{2,1,0:T(8,128)} reshape(f32[524288]{0:T(1024)} %broadcast_multiply_fusion) | data formatting | bytes 4194304 | tf_op jit(solution)/shard_map/mul | solution.py:56
  172.4 1.8 copy.66
  174.2 2.7 %collective-permute-start.4 = (f32[64,32,2]{0,1,2:T(8,128)S(1)}, f32[64,32,2]{0,1,2:T(8,128)S(1)}, u32[]{:S(2)}, u32[]{:S(2)}) collective-permute-start(f32[64,32,2]{0,1,2:T(8,128)S(1)} %copy.66), channel_id=1, source_target_pairs={{8,0},{16,8},{24,16},{0,24},{9,1},{17,9},{25,17},{1,25},{10,2},{18... | collective-permute-start | bytes 49160 | tf_op jit(solution)/shard_map/ppermute | solution.py:27
  179.9 2.9 %collective-permute-done.5 = f32[64,32,2]{0,1,2:T(8,128)S(1)} collective-permute-done((f32[64,32,2]{0,1,2:T(8,128)S(1)}, f32[64,32,2]{0,1,2:T(8,128)S(1)}, u32[]{:S(2)}, u32[]{:S(2)}) %collective-permute-start.5) | collective-permute-done | bytes 16416 | tf_op jit(solution)/shard_map/ppermute | solution.py:26
  182.8 1.8 copy.69
  184.6 2.6 %all-gather.5.cloned.1.call-done = f32[2,64,2,1024]{3,2,1,0:T(2,128)} async-done(((f32[2,64,2,256]{3,2,1,0:T(2,128)}), f32[2,64,2,1024]{3,2,1,0:T(2,128)}) %all-gather.5.cloned.1.call-update) | async-done | bytes 1048592 | tf_op jit(solution)/shard_map/all_gather | solution.py:61
  187.2 1.5 constant_dynamic-update-slice_fusion.3
  188.7 1.5 constant_dynamic-update-slice_fusion.2
  192.3 7.7 %fusion.25 = f32[64,32,256]{2,1,0:T(8,128)} fusion(f32[64,32,256]{2,1,0:T(8,128)S(1)} %copy-done.3, f32[64,32,256]{2,1,0:T(8,128)S(1)} %copy-done.6, f32[2,32,256]{2,1,0:T(8,128)S(1)} %get-tuple-element.13, f32[2,32,256]{2,1,0:T(8,128)S(1)} %get-tuple-element.12, f32[64,2,256]{2,1,0:T(2,128)S(1)} %dynamic-slice_bitcast_fusion.1, ...), kind=kLoop, calls=%fused_computation.59 | loop fusion | flops 33554432 | bytes 11960448 | tf_op jit(solution)/shard_map/add | solution.py:126
  (92 shorter events, 27.0 us)
Async XLA Ops:
  8.5 81.4 %collective-permute-start.2 = (f32[64,2,256]{2,1,0:T(2,128)S(1)}, f32[64,2,256]{2,1,0:T(2,128)S(1)}, u32[]{:S(2)}, u32[]{:S(2)}) collective-permute-start(f32[64,2,256]{2,1,0:T(2,128)S(1)} %get-tuple-element.18), channel_id=1, source_target_pairs={{0,1},{1,2},{2,3},{3,4},{4,5},{5,6},{6,7},{7,0},{8,9},{9,10},{10,1... | collective-permute-start | bytes 393224 | tf_op jit(solution)/shard_map/ppermute | solution.py:26
  9.0 80.9 %collective-permute-start.3 = (f32[64,2,256]{2,1,0:T(2,128)S(1)}, f32[64,2,256]{2,1,0:T(2,128)S(1)}, u32[]{:S(2)}, u32[]{:S(2)}) collective-permute-start(f32[64,2,256]{2,1,0:T(2,128)S(1)} %get-tuple-element.19), channel_id=1, source_target_pairs={{1,0},{2,1},{3,2},{4,3},{5,4},{6,5},{7,6},{0,7},{9,8},{10,9},{11,1... | collective-permute-start | bytes 393224 | tf_op jit(solution)/shard_map/ppermute | solution.py:27
  13.1 17.8 %all-to-all-start = ((s32[1,32,64]{2,0,1:T(1,128)}), s32[1,32,64]{2,0,1:T(1,128)S(1)}, u32[]{:S(2)}, u32[]{:S(2)}) async-start(s32[1,32,64]{2,0,1:T(1,128)} %bitcast.101), calls=%async_computation | async-start | bytes 32768 | tf_op jit(solution)/shard_map/all_to_all | solution.py:71
  19.5 4.9 %copy-start.13 = (s32[2]{0:T(128)S(1)}, s32[2]{0:T(128)}, u32[]{:S(2)}) copy-start(s32[2]{0:T(128)} %param.10) | copy-start | bytes 28
  19.5 5.5 %copy-start.11 = (f32[1,32,64]{2,1,0:T(8,128)S(1)}, f32[1,32,64]{2,1,0:T(8,128)}, u32[]{:S(2)}) copy-start(f32[1,32,64]{2,1,0:T(8,128)} %param.12) | copy-start | bytes 24580
  19.5 5.5 %copy-start.12 = (s32[1,32]{1,0:T(1,128)S(1)}, s32[1,32]{1,0:T(1,128)}, u32[]{:S(2)}) copy-start(s32[1,32]{1,0:T(1,128)} %param.15) | copy-start | bytes 388
  20.2 74.0 %collective-permute-start = (f32[64,32,2]{0,1,2:T(8,128)S(1)}, f32[64,32,2]{0,1,2:T(8,128)S(1)}, u32[]{:S(2)}, u32[]{:S(2)}) collective-permute-start(f32[64,32,2]{0,1,2:T(8,128)S(1)} %copy.73), channel_id=1, source_target_pairs={{8,0},{16,8},{24,16},{0,24},{9,1},{17,9},{25,17},{1,25},{10,2},{18... | collective-permute-start | bytes 49160 | tf_op jit(solution)/shard_map/ppermute | solution.py:27
  23.5 71.7 %collective-permute-start.1 = (f32[64,32,2]{0,1,2:T(8,128)S(1)}, f32[64,32,2]{0,1,2:T(8,128)S(1)}, u32[]{:S(2)}, u32[]{:S(2)}) collective-permute-start(f32[64,32,2]{0,1,2:T(8,128)S(1)} %copy.74), channel_id=1, source_target_pairs={{0,8},{8,16},{16,24},{24,0},{1,9},{9,17},{17,25},{25,1},{2,10},{10... | collective-permute-start | bytes 49160 | tf_op jit(solution)/shard_map/ppermute | solution.py:26
  30.9 13.2 %all-to-all-start.1 = ((f32[1,32,64]{2,0,1:T(1,128)}), f32[1,32,64]{2,0,1:T(1,128)S(1)}, u32[]{:S(2)}, u32[]{:S(2)}) async-start(f32[1,32,64]{2,0,1:T(1,128)} %bitcast.11), calls=%async_computation.1 | async-start | bytes 32768 | tf_op jit(solution)/shard_map/all_to_all | solution.py:115
  44.1 9.6 %all-to-all-start.2 = ((f32[1,32,64]{2,0,1:T(1,128)}), f32[1,32,64]{2,0,1:T(1,128)S(1)}, u32[]{:S(2)}, u32[]{:S(2)}) async-start(f32[1,32,64]{2,0,1:T(1,128)} %bitcast.12), calls=%async_computation.2 | async-start | bytes 32768 | tf_op jit(solution)/shard_map/all_to_all | solution.py:114
  67.6 15.0 %copy-start.10 = (f32[1,32,64]{2,1,0:T(8,128)S(1)}, f32[1,32,64]{2,1,0:T(8,128)}, u32[]{:S(2)}) copy-start(f32[1,32,64]{2,1,0:T(8,128)} %param.13) | copy-start | bytes 24580
  68.3 14.3 %all-to-all-start.3 = ((f32[32,1,64]{2,1,0:T(1,128)}), f32[32,1,64]{2,1,0:T(1,128)S(1)}, u32[]{:S(2)}, u32[]{:S(2)}) async-start(f32[32,1,64]{2,1,0:T(1,128)} %bitcast.23), calls=%async_computation.3 | async-start | bytes 32768 | tf_op jit(solution)/shard_map/all_to_all | solution.py:75
  84.0 13.0 %all-to-all-start.4 = ((f32[1,32,64]{2,0,1:T(1,128)}), f32[1,32,64]{2,0,1:T(1,128)S(1)}, u32[]{:S(2)}, u32[]{:S(2)}) async-start(f32[1,32,64]{2,0,1:T(1,128)} %bitcast.25), calls=%async_computation.4 | async-start | bytes 32768 | tf_op jit(solution)/shard_map/all_to_all | solution.py:123
  89.8 30.4 %all-gather.3.cloned.1.call-start = ((), (), s32[]{:S(2)}) async-start(), calls=%async_computation.6 | async-start | bytes 1310720 | tf_op jit(solution)/shard_map/all_gather | solution.py:61
  90.7 96.4 %all-gather.5.cloned.1.call-start = ((), (), s32[]{:S(2)}) async-start(), calls=%async_computation.7 | async-start | bytes 1310720 | tf_op jit(solution)/shard_map/all_gather | solution.py:61
  120.2 1.5 copy-start.8
  121.8 1.9 copy-start.4
  121.9 2.4 %copy-start = (f32[64,32,256]{2,1,0:T(8,128)S(1)}, f32[64,32,256]{2,1,0:T(8,128)}, u32[]{:S(2)}) copy-start(f32[64,32,256]{2,1,0:T(8,128)} %param.8) | copy-start | bytes 6291460
  122.0 2.7 %copy-start.7 = (f32[64,32,2]{2,1,0:T(8,128)S(1)}, f32[64,32,2]{2,1,0:T(8,128)}, u32[]{:S(2)}) copy-start(f32[64,32,2]{2,1,0:T(8,128)} %copy.62) | copy-start | bytes 49156
  131.3 4.8 %copy-start.2 = (f32[64,32,256]{2,1,0:T(8,128)}, f32[64,32,256]{2,1,0:T(8,128)S(1)}, u32[]{:S(2)}) copy-start(f32[64,32,256]{2,1,0:T(8,128)S(1)} %fusion.18) | copy-start | bytes 6291460
  131.4 29.2 %collective-permute-start.6 = (f32[64,2,256]{2,1,0:T(2,128)S(1)}, f32[64,2,256]{2,1,0:T(2,128)S(1)}, u32[]{:S(2)}, u32[]{:S(2)}) collective-permute-start(f32[64,2,256]{2,1,0:T(2,128)S(1)} %get-tuple-element.10), channel_id=1, source_target_pairs={{0,1},{1,2},{2,3},{3,4},{4,5},{5,6},{6,7},{7,0},{8,9},{9,10},{10,1... | collective-permute-start | bytes 393224 | tf_op jit(solution)/shard_map/ppermute | solution.py:26
  131.5 29.1 %collective-permute-start.7 = (f32[64,2,256]{2,1,0:T(2,128)S(1)}, f32[64,2,256]{2,1,0:T(2,128)S(1)}, u32[]{:S(2)}, u32[]{:S(2)}) collective-permute-start(f32[64,2,256]{2,1,0:T(2,128)S(1)} %get-tuple-element.11), channel_id=1, source_target_pairs={{1,0},{2,1},{3,2},{4,3},{5,4},{6,5},{7,6},{0,7},{9,8},{10,9},{11,1... | collective-permute-start | bytes 393224 | tf_op jit(solution)/shard_map/ppermute | solution.py:27
  161.4 6.8 %copy-start.3 = (f32[64,32,256]{2,1,0:T(8,128)S(1)}, f32[64,32,256]{2,1,0:T(8,128)}, u32[]{:S(2)}) copy-start(f32[64,32,256]{2,1,0:T(8,128)} %copy-done.2) | copy-start | bytes 6291460
  165.4 12.1 %all-to-all-start.5 = ((f32[32,1,64]{2,1,0:T(1,128)}), f32[32,1,64]{2,1,0:T(1,128)S(1)}, u32[]{:S(2)}, u32[]{:S(2)}) async-start(f32[32,1,64]{2,1,0:T(1,128)} %bitcast.27), calls=%async_computation.5 | async-start | bytes 32768 | tf_op jit(solution)/shard_map/all_to_all | solution.py:75
  174.2 4.7 %collective-permute-start.4 = (f32[64,32,2]{0,1,2:T(8,128)S(1)}, f32[64,32,2]{0,1,2:T(8,128)S(1)}, u32[]{:S(2)}, u32[]{:S(2)}) collective-permute-start(f32[64,32,2]{0,1,2:T(8,128)S(1)} %copy.66), channel_id=1, source_target_pairs={{8,0},{16,8},{24,16},{0,24},{9,1},{17,9},{25,17},{1,25},{10,2},{18... | collective-permute-start | bytes 49160 | tf_op jit(solution)/shard_map/ppermute | solution.py:27
  177.5 5.3 %collective-permute-start.5 = (f32[64,32,2]{0,1,2:T(8,128)S(1)}, f32[64,32,2]{0,1,2:T(8,128)S(1)}, u32[]{:S(2)}, u32[]{:S(2)}) collective-permute-start(f32[64,32,2]{0,1,2:T(8,128)S(1)} %copy.68), channel_id=1, source_target_pairs={{0,8},{8,16},{16,24},{24,0},{1,9},{9,17},{17,25},{25,1},{2,10},{10... | collective-permute-start | bytes 49160 | tf_op jit(solution)/shard_map/ppermute | solution.py:26
  187.2 3.7 %copy-start.6 = (f32[64,32,256]{2,1,0:T(8,128)S(1)}, f32[64,32,256]{2,1,0:T(8,128)}, u32[]{:S(2)}) copy-start(f32[64,32,256]{2,1,0:T(8,128)} %mul.192) | copy-start | bytes 6291460
  188.7 2.3 %copy-start.5 = (bf16[3,64,32,256]{3,2,1,0:T(8,128)(2,1)S(1)}, bf16[3,64,32,256]{3,2,1,0:T(8,128)(2,1)}, u32[]{:S(2)}) copy-start(bf16[3,64,32,256]{3,2,1,0:T(8,128)(2,1)} %param.9) | copy-start | bytes 9437188
  190.2 1.8 copy-start.1
  190.2 2.0 copy-start.9
Sparse Core Ops, SparseCore 0:
  92.5 27.7 all-gather.2
  161.6 25.5 all-gather.4
where the time goes:
time: 207 us
  local copies, waits for them, and re-layouts  58.4 us (28%)
  other arithmetic  52.7 us (25%)
  waiting for transfers between devices  40.6 us (20%)
  starting transfers between devices  38 us (18%)
  between operations  17.1 us (8%)
    all_gather x2, waiting for transfers between devices, shear_move(): gathered = lax.all_gather(ghosts, 'gx', axis=3, tiled=True)  25 us
    scatter-add x2, other arithmetic, field_rhs(): source = jnp.zeros(NZ * CY * CX, jnp.float32).at[cells.reshape(-1)].add(f...  24.5 us
    gather x4, local copies, waits for them, and re-layouts, sample_at(): return field.reshape(-1)[cells]  23.7 us
    ppermute x4, starting transfers between devices, padded(): after = lax.ppermute(leading, axis, down)  13 us
    unnamed x34, local copies, waits for them, and re-layouts  11.6 us
    add x1, other arithmetic, on_device(): 0.75 * scalar_field  7.65 us
    all_to_all x1, waiting for transfers between devices, on_device(): lax.all_to_all(live_coef, ('gx', 'gy'), split_axis=1, concat_axis=0, tile...  6.98 us
    add x1, other arithmetic, on_device(): scalar_field + time_step * field_rhs(scalar_field, shear_offset[0], flux_...  6.65 us
  transfers between devices with their start and end apart: 16, of which 5 were waited for; matrix products, arithmetic and copies ran while one was open for 41% of the time, Pallas kernels for 0%

commit v1 on v0

v1 whole, which is shorter than its diff:
```python
import functools

import jax
import jax.numpy as jnp
from jax import lax
from jax.experimental import pallas as pl
from jax.experimental.pallas import tpu as pltpu
from jax.sharding import PartitionSpec as P

time_step = 0.1
diffusivity = 0.1
mean_speed = 1.0
mean_gradient = 1.0
heat_share = 0.5

MESH = pl.DeviceIdType.MESH
MIB = 1 << 20
BLOCK = 128
WAYS = 4


def halo_kernel(gx_count, gy_count, e_right, e_left, lo, hi, o_left, o_right, y_up, y_low,
                send_x, recv_x, send_lo, recv_up, send_hi, recv_low):
    gx = lax.axis_index("gx")
    gy = lax.axis_index("gy")
    right = lax.rem(gx + 1, gx_count)
    left = lax.rem(gx + gx_count - 1, gx_count)
    first = gy == 0
    last = gy == gy_count - 1

    barrier = pltpu.get_barrier_semaphore()

    def greet(x, y):
        pl.semaphore_signal(barrier, inc=1, device_id=(x, y), device_id_type=MESH)

    greet(right, gy)
    greet(left, gy)

    @pl.when(jnp.logical_not(first))
    def _():
        greet(gx, gy - 1)

    @pl.when(jnp.logical_not(last))
    def _():
        greet(gx, gy + 1)

    @pl.when(first)
    def _():
        for g in range(gx_count):
            greet(g, gy_count - 1)

    @pl.when(last)
    def _():
        for g in range(gx_count):
            greet(g, 0)

    edge = jnp.logical_or(first, last)

    @pl.when(edge)
    def _():
        pl.semaphore_wait(barrier, 3 + gx_count)

    @pl.when(jnp.logical_not(edge))
    def _():
        pl.semaphore_wait(barrier, 4)

    def copy_x(src, dst, k, x):
        return pltpu.make_async_remote_copy(
            src_ref=src, dst_ref=dst, send_sem=send_x.at[k], recv_sem=recv_x.at[k],
            device_id=(x, gy), device_id_type=MESH)

    def copy_lo(g, x, y):
        return pltpu.make_async_remote_copy(
            src_ref=lo, dst_ref=y_up.at[gx], send_sem=send_lo.at[g], recv_sem=recv_up.at[gx],
            device_id=(x, y), device_id_type=MESH)

    def copy_hi(g, x, y):
        return pltpu.make_async_remote_copy(
            src_ref=hi, dst_ref=y_low.at[gx], send_sem=send_hi.at[g], recv_sem=recv_low.at[gx],
            device_id=(x, y), device_id_type=MESH)

    def all_copies(act):
        @pl.when(first)
        def _():
            for g in range(gx_count):
                act(copy_lo(g, g, gy_count - 1))

        @pl.when(last)
        def _():
            for g in range(gx_count):
                act(copy_hi(g, g, 0))

        @pl.when(jnp.logical_not(first))
        def _():
            act(copy_lo(0, gx, gy - 1))

        @pl.when(jnp.logical_not(last))
        def _():
            act(copy_hi(0, gx, gy + 1))

    all_copies(lambda c: c.start())
    to_right = copy_x(e_right, o_left, 0, right)
    to_left = copy_x(e_left, o_right, 1, left)
    to_right.start()
    to_left.start()

    def arrive(rows, slots, sems, s):
        pltpu.make_async_remote_copy(
            src_ref=rows, dst_ref=slots.at[s], send_sem=send_lo.at[0], recv_sem=sems.at[s],
            device_id=(right, gy), device_id_type=MESH).wait_recv()

    @pl.when(last)
    def _():
        for s in range(gx_count):
            arrive(lo, y_up, recv_up, s)

    @pl.when(jnp.logical_not(last))
    def _():
        arrive(lo, y_up, recv_up, gx)

    @pl.when(first)
    def _():
        for s in range(gx_count):
            arrive(hi, y_low, recv_low, s)

    @pl.when(jnp.logical_not(first))
    def _():
        arrive(hi, y_low, recv_low, gx)

    to_right.wait_recv()
    to_left.wait_recv()
    all_copies(lambda c: c.wait_send())
    to_right.wait_send()
    to_left.wait_send()


def halo(which, gx_count, gy_count, e_right, e_left, lo, hi):
    anyspace = pl.BlockSpec(memory_space=pl.ANY)
    sem = pltpu.SemaphoreType.DMA
    f32 = jnp.float32
    return pl.pallas_call(
        functools.partial(halo_kernel, gx_count, gy_count),
        out_shape=[
            jax.ShapeDtypeStruct(e_right.shape, f32),
            jax.ShapeDtypeStruct(e_left.shape, f32),
            jax.ShapeDtypeStruct((gx_count,) + lo.shape, f32),
            jax.ShapeDtypeStruct((gx_count,) + hi.shape, f32),
        ],
        in_specs=[anyspace] * 4,
        out_specs=[anyspace] * 4,
        scratch_shapes=[sem((2,)), sem((2,))] + [sem((gx_count,))] * 4,
        compiler_params=pltpu.CompilerParams(collective_id=which, has_side_effects=True),
        name="halo_%d" % which,
    )(e_right, e_left, lo, hi)


def stencil_kernel(second, dims, full_y, *refs):
    nz, cy, cx = dims
    if second:
        f, vel, o_left, o_right, y_up, y_low, info, f0, q2, out, xe, yg, ring = refs
    else:
        f, vel, o_left, o_right, y_up, y_low, info, out, xe, yg, ring = refs
    gx_count = y_up.shape[0]
    k8 = lax.broadcasted_iota(jnp.int32, (8, 128), 0)
    l8 = lax.broadcasted_iota(jnp.int32, (8, 128), 1)
    hot = ((k8 == 0) & (l8 == 126)) | ((k8 == 1) & (l8 == 127)) | ((k8 == 2) & (l8 == 0)) | ((k8 == 3) & (l8 == 1))
    place = jnp.where(hot, 1.0, 0.0).astype(jnp.float32)
    edges = jnp.concatenate(
        [o_left[...], o_right[...], jnp.zeros((4, nz * cy), jnp.float32)], axis=0)
    xe[...] = lax.dot_general(
        edges, place, (((0,), (0,)), ((), ())), precision=lax.Precision.HIGHEST,
        preferred_element_type=jnp.float32)

    lane = lax.broadcasted_iota(jnp.int32, (nz, cx), 1)
    for src, q_at, base in ((y_up, 0, 0), (y_low, 2, 2)):
        q = info[q_at]
        rem = info[q_at + 1]
        nxt = lax.rem(q + 1, gx_count)
        turn = lax.rem(cx - rem, cx)
        for row in range(2):
            a = pltpu.roll(src[q, row], turn, 1)
            b = pltpu.roll(src[nxt, row], turn, 1)
            yg[base + row] = jnp.where(lane < cx - rem, a, b)

    start = (info[4] * cy).astype(jnp.float32)
    rows = lax.broadcasted_iota(jnp.int32, (cy, cx), 0).astype(jnp.float32) + start
    mean_flow = mean_speed * (2.0 * (rows + 0.5) * (1.0 / full_y) - 1.0)
    c8 = 8.0 / 12.0
    c1 = 1.0 / 12.0
    d16 = diffusivity * 16.0 / 12.0
    d1 = diffusivity / 12.0
    d30 = diffusivity * 90.0 / 12.0

    def plane(z, carry):
        c = f[z]
        zm2 = f[lax.rem(z + nz - 2, nz)]
        zm1 = f[lax.rem(z + nz - 1, nz)]
        zp1 = f[lax.rem(z + 1, nz)]
        zp2 = f[lax.rem(z + 2, nz)]
        ring[0:cy] = c
        ring[cy:cy + 1] = yg[0, pl.ds(z, 1)]
        ring[cy + 1:cy + 2] = yg[1, pl.ds(z, 1)]
        ring[cy + 6:cy + 7] = yg[2, pl.ds(z, 1)]
        ring[cy + 7:cy + 8] = yg[3, pl.ds(z, 1)]
        ry = ring[...]
        ym2 = pltpu.roll(ry, 2, 0)[:cy]
        ym1 = pltpu.roll(ry, 1, 0)[:cy]
        yp1 = pltpu.roll(ry, cy + 7, 0)[:cy]
        yp2 = pltpu.roll(ry, cy + 6, 0)[:cy]
        rx = jnp.concatenate([c, xe[pl.ds(pl.multiple_of(z * cy, cy), cy)]], axis=1)
        wide = cx + 128
        xm2 = pltpu.roll(rx, 2, 1)[:, :cx]
        xm1 = pltpu.roll(rx, 1, 1)[:, :cx]
        xp1 = pltpu.roll(rx, wide - 1, 1)[:, :cx]
        xp2 = pltpu.roll(rx, wide - 2, 1)[:, :cx]
        u = vel[0, z].astype(jnp.float32) + mean_flow
        v = vel[1, z].astype(jnp.float32)
        w = vel[2, z].astype(jnp.float32)
        gx_ = c8 * (xp1 - xm1) - c1 * (xp2 - xm2)
        gy_ = c8 * (yp1 - ym1) - c1 * (yp2 - ym2)
        gz_ = c8 * (zp1 - zm1) - c1 * (zp2 - zm2)
        near = ((xp1 + xm1) + (yp1 + ym1)) + (zp1 + zm1)
        far = ((xp2 + xm2) + (yp2 + ym2)) + (zp2 + zm2)
        rhs = (d16 * near - d1 * far - d30 * c) - u * gx_ - v * (gy_ + mean_gradient) - w * gz_
        euler = c + time_step * rhs
        if second:
            out[z] = 0.75 * f0[z] + 0.25 * euler + q2[pl.ds(pl.multiple_of(z * cy, cy), cy)]
        else:
            out[z] = euler
        return carry

    lax.fori_loop(0, nz, plane, 0, unroll=2)


def stencil(second, full_y, f, vel, o_left, o_right, y_up, y_low, info, *more):
    nz, cy, cx = f.shape
    vm = pl.BlockSpec(memory_space=pltpu.VMEM)
    return pl.pallas_call(
        functools.partial(stencil_kernel, second, (nz, cy, cx), full_y),
        out_shape=jax.ShapeDtypeStruct((nz, cy, cx), jnp.float32),
        in_specs=[vm] * 6 + [pl.BlockSpec(memory_space=pltpu.SMEM)] + [vm] * len(more),
        out_specs=vm,
        scratch_shapes=[
            pltpu.VMEM((nz * cy, 128), jnp.float32),
            pltpu.VMEM((4, nz, cx), jnp.float32),
            pltpu.VMEM((cy + 8, cx), jnp.float32),
        ],
        compiler_params=pltpu.CompilerParams(vmem_limit_bytes=32 * MIB),
        cost_estimate=pl.CostEstimate(flops=70 * nz * cy * cx, bytes_accessed=10 * MIB, transcendentals=0),
        name="stencil_two" if second else "stencil_one",
    )(f, vel, o_left, o_right, y_up, y_low, info, *more)


def particle_kernel(second, dims, *refs):
    nz, cy, cx = dims
    if second:
        rows, pack, field, out, packed, buf, acc1, acc2, acc3 = refs
        scale = 0.25 * time_step * heat_share
    else:
        rows, pack, field, base, out, packed, e_right, e_left, lo, hi, buf, acc1, acc2, acc3 = refs
        scale = time_step * heat_share
    accs = (out, acc1, acc2, acc3)
    cells = nz * cy
    blocks = pack.shape[1] // BLOCK

    def clear(i, carry):
        at = pl.ds(pl.multiple_of(i * 64, 64), 64)
        zero = jnp.zeros((64, cx), jnp.float32)
        out[at] = zero if second else base[at]
        for acc in accs[1:]:
            acc[at] = zero
        return carry

    lax.fori_loop(0, cells // 64, clear, 0)
    lane = lax.broadcasted_iota(jnp.int32, (BLOCK, cx), 1)
    lane8 = lax.broadcasted_iota(jnp.int32, (BLOCK, 8), 1)

    def block(b, carry):
        at = pl.multiple_of(b * BLOCK, BLOCK)
        for i in range(BLOCK):
            buf[i:i + 1] = field[pl.ds(rows[at + i], 1)]
        t = pack[:, pl.ds(at, BLOCK)].T
        hit = lane == t[:, 0:1].astype(jnp.int32)
        sample = jnp.sum(jnp.where(hit, buf[...], 0.0), axis=1, keepdims=True)
        now = t[:, 4:5]
        flux = t[:, 2:3] * (now - sample)
        nxt = now + time_step * (t[:, 3:4] - flux)
        if second:
            nxt = 0.75 * t[:, 1:2] + 0.25 * nxt
        packed[:, pl.ds(at, BLOCK)] = jnp.where(lane8 == 4, nxt, t).T
        buf[...] = jnp.where(hit, scale * flux, 0.0)
        for i in range(0, BLOCK, WAYS):
            ats = [pl.ds(rows[at + i + k], 1) for k in range(WAYS)]
            new = [accs[k][ats[k]] + buf[i + k:i + k + 1] for k in range(WAYS)]
            for k in range(WAYS):
                accs[k][ats[k]] = new[k]
        return carry

    lax.fori_loop(0, blocks, block, 0)

    if second:
        def total(i, carry):
            at = pl.ds(pl.multiple_of(i * 64, 64), 64)
            out[at] = (out[at] + acc1[at]) + (acc2[at] + acc3[at])
            return carry

        lax.fori_loop(0, cells // 64, total, 0)
    else:
        lanes = lax.broadcasted_iota(jnp.int32, (128, 128), 1)

        def total(i, carry):
            at = pl.ds(pl.multiple_of(i * 128, 128), 128)
            new = (out[at] + acc1[at]) + (acc2[at] + acc3[at])
            out[at] = new
            ends = pltpu.roll(jnp.where(lanes < 64, new[:, :128], new[:, cx - 128:]), 2, 1).T
            e_right[:, at] = ends[0:2]
            e_left[:, at] = ends[2:4]
            for k in range(128 // cy):
                z = i * (128 // cy) + k
                for row in range(2):
                    lo[row, pl.ds(z, 1)] = new[k * cy + row:k * cy + row + 1]
                    hi[row, pl.ds(z, 1)] = new[k * cy + cy - 2 + row:k * cy + cy - 1 + row]
            return carry

        lax.fori_loop(0, cells // 128, total, 0)


def particles(second, dims, rows, pack, field, *base):
    nz, cy, cx = dims
    f32 = jnp.float32
    vm = pl.BlockSpec(memory_space=pltpu.VMEM)
    outs = [
        jax.ShapeDtypeStruct((nz * cy, cx), f32),
        jax.ShapeDtypeStruct(pack.shape, f32),
    ]
    if not second:
        outs += [jax.ShapeDtypeStruct((2, nz * cy), f32)] * 2
        outs += [jax.ShapeDtypeStruct((2, nz, cx), f32)] * 2
    grid_space = pltpu.VMEM((nz * cy, cx), f32)
    return pl.pallas_call(
        functools.partial(particle_kernel, second, dims),
        out_shape=outs,
        in_specs=[pl.BlockSpec(memory_space=pltpu.SMEM)] + [vm] * (2 + len(base)),
        out_specs=[vm] * len(outs),
        scratch_shapes=[pltpu.VMEM((BLOCK, cx), f32), grid_space, grid_space, grid_space],
        compiler_params=pltpu.CompilerParams(vmem_limit_bytes=32 * MIB),
        cost_estimate=pl.CostEstimate(flops=20 * MIB, bytes_accessed=10 * MIB, transcendentals=0),
        name="particles_two" if second else "particles_one",
    )(rows, pack, field, *base)


def on_device(
    scalar_field, velocity, shear_offset, part_temp, part_coef, part_heat, part_cell, part_count
):
    nz, cy, cx = scalar_field.shape
    cap = part_temp.shape[2]
    gx_index = lax.axis_index("gx")
    gy_index = lax.axis_index("gy")
    gx_count = lax.axis_size("gx")
    gy_count = lax.axis_size("gy")
    peers = gx_count * gy_count
    full_x = cx * gx_count
    full_y = cy * gy_count
    both = ("gx", "gy")
    live_slot = jnp.arange(cap)[None, None, :] < part_count[:, :, None]
    live_coef = jnp.where(live_slot, part_coef, jnp.float32(0.0))

    send = jnp.concatenate(
        [part_cell.astype(jnp.float32)[0], part_temp[0], live_coef[0], part_heat[0]], axis=1)
    came = lax.all_to_all(send, both, split_axis=0, concat_axis=0, tiled=True)
    came = came.reshape(peers, 4, cap).transpose(1, 0, 2).reshape(4, peers * cap)
    cells = came[0].astype(jnp.int32)
    rows = cells // cx
    pack = jnp.concatenate(
        [(cells % cx).astype(jnp.float32)[None], came[1:], came[1:2],
         jnp.zeros((3, peers * cap), jnp.float32)], axis=0)

    def info(offset):
        low_shift = jnp.where(gy_index == 0, (full_x - offset) % full_x, 0)
        high_shift = jnp.where(gy_index == gy_count - 1, offset, 0)
        up = (gx_index * cx - high_shift) % full_x
        low = (gx_index * cx - low_shift) % full_x
        return jnp.stack([up // cx, up % cx, low // cx, low % cx, gy_index]).astype(jnp.int32)

    def ends(field, at):
        return field[:, :, at:at + 2].reshape(nz * cy, 2).T

    halos = halo(
        0, gx_count, gy_count, ends(scalar_field, cx - 2), ends(scalar_field, 0),
        scalar_field[:, :2].transpose(1, 0, 2), scalar_field[:, cy - 2:].transpose(1, 0, 2))
    base = stencil(False, full_y, scalar_field, velocity, *halos, info(shear_offset[0]))
    flat = (nz * cy, cx)
    dims = (nz, cy, cx)
    section_one, pack, e_right, e_left, lo, hi = particles(
        False, dims, rows, pack, scalar_field.reshape(flat), base.reshape(flat))
    halos = halo(1, gx_count, gy_count, e_right, e_left, lo, hi)
    source, pack = particles(True, dims, rows, pack, section_one)
    home = lax.all_to_all(pack[4].reshape(peers, cap), both, split_axis=0, concat_axis=0, tiled=True)
    scalar_out = stencil(
        True, full_y, section_one.reshape(dims), velocity, *halos, info(shear_offset[1]),
        scalar_field, source)
    temp_out = jnp.where(live_slot, home[None], jnp.float32(0.0))
    return (scalar_out, temp_out)


def solution(mesh):
    in_specs = (
        P(None, "gy", "gx"),
        P(None, None, "gy", "gx"),
        P(),
        P(("gx", "gy"), None, None),
        P(("gx", "gy"), None, None),
        P(("gx", "gy"), None, None),
        P(("gx", "gy"), None, None),
        P(("gx", "gy"), None),
    )
    out_specs = (P(None, "gy", "gx"), P(("gx", "gy"), None, None))
    return jax.shard_map(
        on_device, mesh=mesh, in_specs=in_specs, out_specs=out_specs, check_vma=False
    )
```

time: 207 us -> 126 us (0.61)
  Pallas kernels: 0 us -> 73.1 us
  other arithmetic: 52.7 us -> 3.2 us
  waiting for transfers between devices: 40.6 us -> 0.01 us
  local copies, waits for them, and re-layouts: 58.4 us -> 30.2 us
  starting transfers between devices: 38 us -> 13.7 us
  between operations: 17.1 us -> 3.56 us
    pallas_call x0 -> x6, Pallas kernels: none -> 73.1 us  [the longest x2 31.2 us: particles(): pl.pallas_call(functools.partial(particle_kernel, second, dims), out_shap...]
    all_gather x2 -> x0, waiting for transfers between devices: 25 us -> none  [shear_move(): gathered = lax.all_gather(ghosts, 'gx', axis=3, tiled=True)]
    scatter-add x2 -> x0, other arithmetic: 24.5 us -> none  [field_rhs(): source = jnp.zeros(NZ * CY * CX, jnp.float32).at[cells.reshape(-1)].add(f...]
    gather x4 -> x0, local copies, waits for them, and re-layouts: 23.7 us -> none  [sample_at(): return field.reshape(-1)[cells]]
    add x3 -> x0, other arithmetic: 15.6 us -> none  [the longest x1 7.65 us: on_device(): 0.75 * scalar_field]
    ppermute x8 -> x0, starting transfers between devices: 13.6 us -> none  [the longest x4 13 us: padded(): after = lax.ppermute(leading, axis, down)]
    all_to_all x6 -> x2, waiting for transfers between devices: 12.7 us -> 0.01 us  [the longest x1 0.01 us: on_device(): came = lax.all_to_all(send, both, split_axis=0, concat_axis=0, tiled=True)]
    all_to_all x6 -> x2, starting transfers between devices: 24.3 us -> 13.7 us  [the longest x1 7.3 us: on_device(): came = lax.all_to_all(send, both, split_axis=0, concat_axis=0, tiled=True)]
  transfers between devices with their start and end apart: 16 -> 2, of which waited for: 5 -> 0; matrix products, arithmetic and copies ran while one was open for 41% -> 7% of each run, Pallas kernels for 0% -> 34%
where the time goes in v1:
time: 126 us; the launch traced here: 124 us
  Pallas kernels  73.1 us (58%)
  local copies, waits for them, and re-layouts  30.2 us (24%)
  starting transfers between devices  13.7 us (11%)
  between operations  3.56 us (3%)
  other arithmetic  3.2 us (3%)
    pallas_call x2, Pallas kernels, particles(): pl.pallas_call(functools.partial(particle_kernel, second, dims), out_shap...  31.2 us
    pallas_call x2, Pallas kernels, halo(): pl.pallas_call(functools.partial(halo_kernel, gx_count, gy_count), out_sh...  24.9 us
    unnamed x46, local copies, waits for them, and re-layouts  19.6 us
    pallas_call x2, Pallas kernels, stencil(): pl.pallas_call(functools.partial(stencil_kernel, second, (nz, cy, cx), fu...  17 us
    all_to_all x1, starting transfers between devices, on_device(): came = lax.all_to_all(send, both, split_axis=0, concat_axis=0, tiled=True)  7.3 us
    all_to_all x1, starting transfers between devices, on_device(): lax.all_to_all(pack[4].reshape(peers, cap), both, split_axis=0, concat_ax...  6.39 us
    reshape x2, local copies, waits for them, and re-layouts, ends(): return field[:, :, at:at + 2].reshape(nz * cy, 2).T  3.08 us
    slice x1, local copies, waits for them, and re-layouts, ends(): return field[:, :, at:at + 2].reshape(nz * cy, 2).T  2.88 us
  transfers between devices with their start and end apart: 2, of which 0 were waited for; matrix products, arithmetic and copies ran while one was open for 7% of the time, Pallas kernels for 34%

profile of v1, /device:TPU:0, one launch (start us, length us, event | category | flops | bytes accessed | tf_op | source)
XLA Modules:
  0.0 123.7 jit_solution(16761006366237219306)
XLA Ops:
  0.6 0.7 convert_bitcast_fusion
  1.4 0.8 select_bitcast_fusion
  2.1 0.8 pad_maximum_fusion
  3.6 7.3 %all-to-all-start = ((f32[32,1,256]{2,1,0:T(1,128)}), f32[32,1,256]{2,1,0:T(1,128)S(1)}, u32[]{:S(2)}, u32[]{:S(2)}) async-start(f32[32,1,256]{2,1,0:T(1,128)} %all_to_all.14), calls=%async_computation | async-start | bytes 65536 | tf_op jit(solution)/shard_map/all_to_all | solution.py:370
  10.9 1.3 %fusion.4 = (f32[64,2,256]{2,1,0:T(2,128)S(1)}, f32[64,2,256]{2,1,0:T(2,128)S(1)}) fusion(f32[64,32,256]{2,1,0:T(8,128)} %refs_7_.1), kind=kLoop, calls=%fused_computation.23 | loop fusion | bytes 524288 | tf_op jit(solution)/shard_map/slice | solution.py:390
  12.2 2.9 %fusion.5 = (f32[64,32,2]{2,1,0:T(8,128)}, f32[64,32,2]{2,1,0:T(8,128)S(1)}) fusion(f32[64,32,256]{2,1,0:T(8,128)} %refs_7_.1), kind=kLoop, calls=%fused_computation.24 | loop fusion | bytes 65536 | tf_op jit(solution)/shard_map/slice | solution.py:386
  15.1 0.7 copy_bitcast_fusion
  17.8 2.2 %copy.27 = f32[2048,2]{0,1:T(2,128)} copy(f32[2048,2]{1,0:T(8,128)} %bitcast.40) | data formatting | bytes 32768 | tf_op jit(solution)/shard_map/reshape | solution.py:386
  20.0 0.9 copy.26
  21.0 12.4 %halo_0.1 = (f32[2,2048]{1,0:T(2,128)}, f32[2,2048]{1,0:T(2,128)}, f32[4,2,64,256]{3,2,1,0:T(8,128)}, f32[4,2,64,256]{3,2,1,0:T(8,128)}) custom-call(f32[2,2048]{1,0:T(2,128)} %bitcast.44, f32[2,2048]{1,0:T(2,128)} %bitcast.43, f32[2,64,256]{2,1,0:T(8,128)} %get-tuple-element.43.lo, f32[2,64,256]{2,1,0:T(8,128)} %get-tuple-element.42.hi), custom_call_target="tpu_custom_call" | custom-call | tf_op jit(solution)/shard_map/halo_0/pallas_call | solution.py:141
  33.5 1.9 %copy-done.1 = bf16[3,64,32,256]{3,2,1,0:T(8,128)(2,1)S(1)} copy-done((bf16[3,64,32,256]{3,2,1,0:T(8,128)(2,1)S(1)}, bf16[3,64,32,256]{3,2,1,0:T(8,128)(2,1)}, u32[]{:S(2)}) %copy-start.1) | copy-done | bytes 3145752
  35.4 1.0 copy-done.9
  36.5 1.0 copy-done.10
  37.5 0.7 copy-done.15
  38.2 0.7 copy-done.16
  38.9 7.8 %stencil_one.1 = f32[64,32,256]{2,1,0:T(8,128)S(1)} custom-call(f32[64,32,256]{2,1,0:T(8,128)S(1)} %copy-done, bf16[3,64,32,256]{3,2,1,0:T(8,128)(2,1)S(1)} %copy-done.1, f32[2,2048]{1,0:T(2,128)S(1)} %copy-done.15, f32[2,2048]{1,0:T(2,128)S(1)} %copy-done.16, f32[4,2,64,256]{3,2,1,0:T(8,128)S(1)} %copy-done.9, f32[4,2,64,256]{3,2,1,0:T(8,128)S(1)} %copy-done.10, ...), custom_call_target="tpu_custom_call" | custom-call | flops 36700160 | bytes 10485760 | tf_op jit(solution)/shard_map/stencil_one/pallas_call | solution.py:238
  46.7 1.3 %copy-done.5 = f32[64,32,256]{2,1,0:T(8,128)} copy-done((f32[64,32,256]{2,1,0:T(8,128)}, f32[64,32,256]{2,1,0:T(8,128)S(1)}, u32[]{:S(2)}) %copy-start.5) | copy-done | bytes 2097176
  48.7 1.6 %copy-done.6 = f32[64,32,256]{2,1,0:T(8,128)S(1)} copy-done((f32[64,32,256]{2,1,0:T(8,128)S(1)}, f32[64,32,256]{2,1,0:T(8,128)}, u32[]{:S(2)}) %copy-start.6) | copy-done | bytes 2097176
  50.3 16.3 %particles_one.1 = (f32[2048,256]{1,0:T(8,128)S(1)}, f32[8,2048]{1,0:T(8,128)S(1)}, f32[2,2048]{1,0:T(2,128)S(1)}, f32[2,2048]{1,0:T(2,128)S(1)}, f32[2,64,256]{2,1,0:T(8,128)S(1)}, /*index=5*/f32[2,64,256]{2,1,0:T(8,128)S(1)}) custom-call(s32[2048]{0:T(1024)S(1)} %add_select_fusion.refs_0_, f32[8,2048]{1,0:T(8,128)S(1)} %maximum_maximum_fusion.refs_1_, ...), custom_call_target="tpu_custom_call" | custom-call | flops 20971520 | bytes 10485760 | tf_op jit(solution)/shard_map/particles_one/pallas_call | solution.py:340
  66.7 14.8 %particles_two.1 = (f32[2048,256]{1,0:T(8,128)S(1)}, f32[8,2048]{1,0:T(8,128)S(1)}) custom-call(s32[2048]{0:T(1024)S(1)} %add_select_fusion.refs_0_, f32[8,2048]{1,0:T(8,128)S(1)} %get-tuple-element.31.refs_1_, f32[2048,256]{1,0:T(8,128)S(1)} %get-tuple-element.22.refs_2_), custom_call_target="tpu_custom_call" | custom-call | flops 20971520 | bytes 10485760 | tf_op jit(solution)/shard_map/particles_two/pallas_call | solution.py:340
  81.5 1.3 %copy-done.3 = f32[2048,256]{1,0:T(8,128)} copy-done((f32[2048,256]{1,0:T(8,128)}, f32[2048,256]{1,0:T(8,128)S(1)}, u32[]{:S(2)}) %copy-start.3) | copy-done | bytes 2097176
  82.8 1.4 %copy-done.7 = f32[2048,256]{1,0:T(8,128)} copy-done((f32[2048,256]{1,0:T(8,128)}, f32[2048,256]{1,0:T(8,128)S(1)}, u32[]{:S(2)}) %copy-start.7) | copy-done | bytes 2097176
  84.9 6.4 %all-to-all-start.1 = ((f32[32,1,64]{2,1,0:T(1,128)}), f32[32,1,64]{2,1,0:T(1,128)S(1)}, u32[]{:S(2)}, u32[]{:S(2)}) async-start(f32[32,1,64]{2,1,0:T(1,128)} %bitcast.26), calls=%async_computation.1 | async-start | bytes 32768 | tf_op jit(solution)/shard_map/all_to_all | solution.py:398
  92.7 12.4 %halo_1.1 = (f32[2,2048]{1,0:T(2,128)}, f32[2,2048]{1,0:T(2,128)}, f32[4,2,64,256]{3,2,1,0:T(8,128)}, f32[4,2,64,256]{3,2,1,0:T(8,128)}) custom-call(f32[2,2048]{1,0:T(2,128)} %copy-done.19, f32[2,2048]{1,0:T(2,128)} %copy-done.20, f32[2,64,256]{2,1,0:T(8,128)} %copy-done.13, f32[2,64,256]{2,1,0:T(8,128)} %copy-done.14), custom_call_target="tpu_custom_call" | custom-call | tf_op jit(solution)/shard_map/halo_1/pallas_call | solution.py:141
  105.2 1.9 %copy-done.2 = bf16[3,64,32,256]{3,2,1,0:T(8,128)(2,1)S(1)} copy-done((bf16[3,64,32,256]{3,2,1,0:T(8,128)(2,1)S(1)}, bf16[3,64,32,256]{3,2,1,0:T(8,128)(2,1)}, u32[]{:S(2)}) %copy-start.2) | copy-done | bytes 3145752
  107.1 1.6 %copy-done.4 = f32[2048,256]{1,0:T(8,128)S(1)} copy-done((f32[2048,256]{1,0:T(8,128)S(1)}, f32[2048,256]{1,0:T(8,128)}, u32[]{:S(2)}) %copy-start.4) | copy-done | bytes 2097176
  108.6 1.6 %copy-done.8 = f32[2048,256]{1,0:T(8,128)S(1)} copy-done((f32[2048,256]{1,0:T(8,128)S(1)}, f32[2048,256]{1,0:T(8,128)}, u32[]{:S(2)}) %copy-start.8) | copy-done | bytes 2097176
  110.2 1.0 copy-done.11
  111.3 1.0 copy-done.12
  112.3 0.7 copy-done.17
  113.0 0.7 copy-done.18
  113.8 9.3 %stencil_two.1 = f32[64,32,256]{2,1,0:T(8,128)} custom-call(f32[64,32,256]{2,1,0:T(8,128)S(1)} %bitcast.37, bf16[3,64,32,256]{3,2,1,0:T(8,128)(2,1)S(1)} %copy-done.2, f32[2,2048]{1,0:T(2,128)S(1)} %copy-done.17, f32[2,2048]{1,0:T(2,128)S(1)} %copy-done.18, f32[4,2,64,256]{3,2,1,0:T(8,128)S(1)} %copy-done.11, f32[4,2,64,256]{3,2,1,0:T(8,128)S(1)} %copy-done.12, ...), custom_call_target="tpu_custom_call" | custom-call | flops 36700160 | bytes 10485760 | tf_op jit(solution)/shard_map/stencil_two/pallas_call | solution.py:238
  (53 shorter events, 3.6 us)
Async XLA Ops:
  3.6 44.4 %all-to-all-start = ((f32[32,1,256]{2,1,0:T(1,128)}), f32[32,1,256]{2,1,0:T(1,128)S(1)}, u32[]{:S(2)}, u32[]{:S(2)}) async-start(f32[32,1,256]{2,1,0:T(1,128)} %all_to_all.14), calls=%async_computation | async-start | bytes 65536 | tf_op jit(solution)/shard_map/all_to_all | solution.py:370
  12.2 3.6 %copy-start.22 = (s32[2]{0:T(128)S(1)}, s32[2]{0:T(128)}, u32[]{:S(2)}) copy-start(s32[2]{0:T(128)} %param.10) | copy-start | bytes 28
  15.1 18.4 %copy-start = (f32[64,32,256]{2,1,0:T(8,128)S(1)}, f32[64,32,256]{2,1,0:T(8,128)}, u32[]{:S(2)}) copy-start(f32[64,32,256]{2,1,0:T(8,128)} %refs_7_.1) | copy-start | bytes 6291460
  33.5 1.9 %copy-start.1 = (bf16[3,64,32,256]{3,2,1,0:T(8,128)(2,1)S(1)}, bf16[3,64,32,256]{3,2,1,0:T(8,128)(2,1)}, u32[]{:S(2)}) copy-start(bf16[3,64,32,256]{3,2,1,0:T(8,128)(2,1)} %refs_1_.3) | copy-start | bytes 9437188
  35.4 1.0 copy-start.9
  36.5 1.0 copy-start.10
  37.5 0.7 copy-start.15
  38.2 0.7 copy-start.16
  46.7 1.3 %copy-start.5 = (f32[64,32,256]{2,1,0:T(8,128)}, f32[64,32,256]{2,1,0:T(8,128)S(1)}, u32[]{:S(2)}) copy-start(f32[64,32,256]{2,1,0:T(8,128)S(1)} %stencil_one.1) | copy-start | bytes 6291460
  48.7 1.6 %copy-start.6 = (f32[64,32,256]{2,1,0:T(8,128)S(1)}, f32[64,32,256]{2,1,0:T(8,128)}, u32[]{:S(2)}) copy-start(f32[64,32,256]{2,1,0:T(8,128)} %copy-done.5) | copy-start | bytes 6291460
  66.6 14.9 %copy-start.13 = (f32[2,64,256]{2,1,0:T(8,128)}, f32[2,64,256]{2,1,0:T(8,128)S(1)}, u32[]{:S(2)}) copy-start(f32[2,64,256]{2,1,0:T(8,128)S(1)} %get-tuple-element.25.lo) | copy-start | bytes 393220
  66.6 17.6 %copy-start.14 = (f32[2,64,256]{2,1,0:T(8,128)}, f32[2,64,256]{2,1,0:T(8,128)S(1)}, u32[]{:S(2)}) copy-start(f32[2,64,256]{2,1,0:T(8,128)S(1)} %get-tuple-element.26.hi) | copy-start | bytes 393220
  66.6 17.6 %copy-start.19 = (f32[2,2048]{1,0:T(2,128)}, f32[2,2048]{1,0:T(2,128)S(1)}, u32[]{:S(2)}) copy-start(f32[2,2048]{1,0:T(2,128)S(1)} %get-tuple-element.23.e_right) | copy-start | bytes 49156
  66.6 17.6 %copy-start.20 = (f32[2,2048]{1,0:T(2,128)}, f32[2,2048]{1,0:T(2,128)S(1)}, u32[]{:S(2)}) copy-start(f32[2,2048]{1,0:T(2,128)S(1)} %get-tuple-element.24.e_left) | copy-start | bytes 49156
  81.5 1.3 %copy-start.3 = (f32[2048,256]{1,0:T(8,128)}, f32[2048,256]{1,0:T(8,128)S(1)}, u32[]{:S(2)}) copy-start(f32[2048,256]{1,0:T(8,128)S(1)} %get-tuple-element.22.refs_2_) | copy-start | bytes 6291460
  82.8 1.4 %copy-start.7 = (f32[2048,256]{1,0:T(8,128)}, f32[2048,256]{1,0:T(8,128)S(1)}, u32[]{:S(2)}) copy-start(f32[2048,256]{1,0:T(8,128)S(1)} %get-tuple-element.32.refs_8_) | copy-start | bytes 6291460
  84.9 38.1 %all-to-all-start.1 = ((f32[32,1,64]{2,1,0:T(1,128)}), f32[32,1,64]{2,1,0:T(1,128)S(1)}, u32[]{:S(2)}, u32[]{:S(2)}) async-start(f32[32,1,64]{2,1,0:T(1,128)} %bitcast.26), calls=%async_computation.1 | async-start | bytes 32768 | tf_op jit(solution)/shard_map/all_to_all | solution.py:398
  105.2 1.9 %copy-start.2 = (bf16[3,64,32,256]{3,2,1,0:T(8,128)(2,1)S(1)}, bf16[3,64,32,256]{3,2,1,0:T(8,128)(2,1)}, u32[]{:S(2)}) copy-start(bf16[3,64,32,256]{3,2,1,0:T(8,128)(2,1)} %refs_1_.3) | copy-start | bytes 9437188
  107.1 1.6 %copy-start.4 = (f32[2048,256]{1,0:T(8,128)S(1)}, f32[2048,256]{1,0:T(8,128)}, u32[]{:S(2)}) copy-start(f32[2048,256]{1,0:T(8,128)} %copy-done.3) | copy-start | bytes 6291460
  108.6 1.6 %copy-start.8 = (f32[2048,256]{1,0:T(8,128)S(1)}, f32[2048,256]{1,0:T(8,128)}, u32[]{:S(2)}) copy-start(f32[2048,256]{1,0:T(8,128)} %copy-done.7) | copy-start | bytes 6291460
  110.2 1.0 copy-start.11
  111.3 1.0 copy-start.12
  112.3 0.7 copy-start.17
  113.0 0.7 copy-start.18
  113.8 9.3 %copy-start.21 = (s32[1,32]{1,0:T(1,128)S(1)}, s32[1,32]{1,0:T(1,128)}, u32[]{:S(2)}) copy-start(s32[1,32]{1,0:T(1,128)} %param.15) | copy-start | bytes 388

commit v2 on v1

v2 whole, which is shorter than its diff:
```python
import functools

import jax
import jax.numpy as jnp
from jax import lax
from jax.experimental import pallas as pl
from jax.experimental.pallas import tpu as pltpu
from jax.sharding import PartitionSpec as P

time_step = 0.1
diffusivity = 0.1
mean_speed = 1.0
mean_gradient = 1.0
heat_share = 0.5

MESH = pl.DeviceIdType.MESH
MIB = 1 << 20
GROUP = 4
LANES = 128
WAYS = 4


def exchange_kernel(gx_count, gy_count, e_right, e_left, lo, hi, mail, o_left, o_right, y_up, y_low, came,
                    send_x, recv_x, send_lo, recv_up, send_hi, recv_low, send_p, recv_p, own_sem):
    gx = lax.axis_index("gx")
    gy = lax.axis_index("gy")
    right = lax.rem(gx + 1, gx_count)
    left = lax.rem(gx + gx_count - 1, gx_count)
    first = gy == 0
    last = gy == gy_count - 1

    barrier = pltpu.get_barrier_semaphore()

    peers = gx_count * gy_count
    me = gx * gy_count + gy

    def peer(i):
        d = lax.rem(me + i, peers)
        return d, (d // gy_count, lax.rem(d, gy_count))

    def greet(i, carry):
        pl.semaphore_signal(barrier, inc=1, device_id=peer(i)[1], device_id_type=MESH)
        return carry

    lax.fori_loop(1, peers, greet, 0)
    own = pltpu.make_async_copy(mail.at[me], came.at[me], own_sem)
    own.start()
    pl.semaphore_wait(barrier, peers - 1)

    def copy_mail(i):
        d, place = peer(i)
        return pltpu.make_async_remote_copy(
            src_ref=mail.at[d], dst_ref=came.at[me], send_sem=send_p.at[d], recv_sem=recv_p.at[me],
            device_id=place, device_id_type=MESH)

    def copy_x(src, dst, k, x):
        return pltpu.make_async_remote_copy(
            src_ref=src, dst_ref=dst, send_sem=send_x.at[k], recv_sem=recv_x.at[k],
            device_id=(x, gy), device_id_type=MESH)

    def copy_lo(g, x, y):
        return pltpu.make_async_remote_copy(
            src_ref=lo, dst_ref=y_up.at[gx], send_sem=send_lo.at[g], recv_sem=recv_up.at[gx],
            device_id=(x, y), device_id_type=MESH)

    def copy_hi(g, x, y):
        return pltpu.make_async_remote_copy(
            src_ref=hi, dst_ref=y_low.at[gx], send_sem=send_hi.at[g], recv_sem=recv_low.at[gx],
            device_id=(x, y), device_id_type=MESH)

    def all_copies(act):
        @pl.when(first)
        def _():
            for g in range(gx_count):
                act(copy_lo(g, g, gy_count - 1))

        @pl.when(last)
        def _():
            for g in range(gx_count):
                act(copy_hi(g, g, 0))

        @pl.when(jnp.logical_not(first))
        def _():
            act(copy_lo(0, gx, gy - 1))

        @pl.when(jnp.logical_not(last))
        def _():
            act(copy_hi(0, gx, gy + 1))

    all_copies(lambda c: c.start())
    to_right = copy_x(e_right, o_left, 0, right)
    to_left = copy_x(e_left, o_right, 1, left)
    to_right.start()
    to_left.start()

    def post(i, carry):
        copy_mail(i).start()
        return carry

    lax.fori_loop(1, peers, post, 0)

    def arrive(rows, slots, sems, s):
        pltpu.make_async_remote_copy(
            src_ref=rows, dst_ref=slots.at[s], send_sem=send_lo.at[0], recv_sem=sems.at[s],
            device_id=(right, gy), device_id_type=MESH).wait_recv()

    @pl.when(last)
    def _():
        for s in range(gx_count):
            arrive(lo, y_up, recv_up, s)

    @pl.when(jnp.logical_not(last))
    def _():
        arrive(lo, y_up, recv_up, gx)

    @pl.when(first)
    def _():
        for s in range(gx_count):
            arrive(hi, y_low, recv_low, s)

    @pl.when(jnp.logical_not(first))
    def _():
        arrive(hi, y_low, recv_low, gx)

    to_right.wait_recv()
    to_left.wait_recv()
    all_copies(lambda c: c.wait_send())
    to_right.wait_send()
    to_left.wait_send()

    def finish(i, carry):
        d, place = peer(i)
        copy = pltpu.make_async_remote_copy(
            src_ref=mail.at[d], dst_ref=came.at[d], send_sem=send_p.at[d], recv_sem=recv_p.at[d],
            device_id=place, device_id_type=MESH)
        copy.wait_recv()
        copy.wait_send()
        return carry

    lax.fori_loop(1, peers, finish, 0)
    own.wait()


def exchange(which, gx_count, gy_count, e_right, e_left, lo, hi, mail):
    vm = pl.BlockSpec(memory_space=pltpu.VMEM)
    sem = pltpu.SemaphoreType.DMA
    f32 = jnp.float32
    peers = gx_count * gy_count
    return pl.pallas_call(
        functools.partial(exchange_kernel, gx_count, gy_count),
        out_shape=[
            jax.ShapeDtypeStruct(e_right.shape, f32),
            jax.ShapeDtypeStruct(e_left.shape, f32),
            jax.ShapeDtypeStruct((gx_count,) + lo.shape, f32),
            jax.ShapeDtypeStruct((gx_count,) + hi.shape, f32),
            jax.ShapeDtypeStruct(mail.shape, f32),
        ],
        in_specs=[vm] * 5,
        out_specs=[vm] * 5,
        scratch_shapes=[sem((2,)), sem((2,))] + [sem((gx_count,))] * 4 + [sem((peers,)), sem((peers,)), sem],
        compiler_params=pltpu.CompilerParams(
            collective_id=which, has_side_effects=True, vmem_limit_bytes=8 * MIB),
        name="exchange_%d" % which,
    )(e_right, e_left, lo, hi, mail)


def column(count):
    peers = count.shape[1]
    return jnp.broadcast_to(count.astype(jnp.float32), (8, peers)).T[:, 0:1].astype(jnp.int32)


def put_ends(new, i, dims, e_right, e_left, lo, hi):
    nz, cy, cx = dims
    at = pl.ds(pl.multiple_of(i * 128, 128), 128)
    lanes = lax.broadcasted_iota(jnp.int32, (128, 128), 1)
    ends = pltpu.roll(jnp.where(lanes < 64, new[:, :128], new[:, cx - 128:]), 2, 1).T
    e_right[:, at] = ends[0:2]
    e_left[:, at] = ends[2:4]
    for k in range(128 // cy):
        z = i * (128 // cy) + k
        for row in range(2):
            lo[row, pl.ds(z, 1)] = new[k * cy + row:k * cy + row + 1]
            hi[row, pl.ds(z, 1)] = new[k * cy + cy - 2 + row:k * cy + cy - 1 + row]


def prepare_kernel(dims, f, cell, temp, coef, heat, count, e_right, e_left, lo, hi, mail):
    nz, cy, cx = dims
    slot = lax.broadcasted_iota(jnp.int32, coef.shape[1:], 1)
    live = jnp.where(slot < column(count[...]), coef[0], 0.0)
    mail[:, 0, :] = jnp.concatenate([cell[0].astype(jnp.float32), temp[0]], axis=1)
    mail[:, 1, :] = jnp.concatenate([live, heat[0]], axis=1)

    def part(i, carry):
        put_ends(f[pl.ds(pl.multiple_of(i * 128, 128), 128)], i, dims, e_right, e_left, lo, hi)
        return carry

    lax.fori_loop(0, nz * cy // 128, part, 0)


def ends_shapes(dims):
    nz, cy, cx = dims
    return ([jax.ShapeDtypeStruct((2, nz * cy), jnp.float32)] * 2
            + [jax.ShapeDtypeStruct((2, nz, cx), jnp.float32)] * 2)


def prepare(dims, f, cell, temp, coef, heat, count):
    vm = pl.BlockSpec(memory_space=pltpu.VMEM)
    peers, cap = cell.shape[1:]
    return pl.pallas_call(
        functools.partial(prepare_kernel, dims),
        out_shape=ends_shapes(dims) + [jax.ShapeDtypeStruct((peers, 2, 2 * cap), jnp.float32)],
        in_specs=[vm] * 6,
        out_specs=[vm] * 5,
        compiler_params=pltpu.CompilerParams(vmem_limit_bytes=8 * MIB),
        name="prepare",
    )(f, cell, temp, coef, heat, count)


def stencil(dims, full_y, f, vel, o_left, o_right, y_up, y_low, info, xe, yg, ring, store):
    nz, cy, cx = dims
    gx_count = y_up.shape[0]
    k8 = lax.broadcasted_iota(jnp.int32, (8, 128), 0)
    l8 = lax.broadcasted_iota(jnp.int32, (8, 128), 1)
    hot = ((k8 == 0) & (l8 == 126)) | ((k8 == 1) & (l8 == 127)) | ((k8 == 2) & (l8 == 0)) | ((k8 == 3) & (l8 == 1))
    place = jnp.where(hot, 1.0, 0.0).astype(jnp.float32)
    edges = jnp.concatenate(
        [o_left[...], o_right[...], jnp.zeros((4, nz * cy), jnp.float32)], axis=0)
    xe[...] = lax.dot_general(
        edges, place, (((0,), (0,)), ((), ())), precision=lax.Precision.HIGHEST,
        preferred_element_type=jnp.float32)

    lane = lax.broadcasted_iota(jnp.int32, (nz, cx), 1)
    for src, q_at, base in ((y_up, 0, 0), (y_low, 2, 2)):
        q = info[q_at]
        rem = info[q_at + 1]
        nxt = lax.rem(q + 1, gx_count)
        turn = lax.rem(cx - rem, cx)
        for row in range(2):
            a = pltpu.roll(src[q, row], turn, 1)
            b = pltpu.roll(src[nxt, row], turn, 1)
            yg[base + row] = jnp.where(lane < cx - rem, a, b)

    start = (info[4] * cy).astype(jnp.float32)
    rows = lax.broadcasted_iota(jnp.int32, (cy, cx), 0).astype(jnp.float32) + start
    mean_flow = mean_speed * (2.0 * (rows + 0.5) * (1.0 / full_y) - 1.0)
    c8 = 8.0 / 12.0
    c1 = 1.0 / 12.0
    d16 = diffusivity * 16.0 / 12.0
    d1 = diffusivity / 12.0
    d30 = diffusivity * 90.0 / 12.0

    def plane(z, carry):
        c = f[pl.ds(pl.multiple_of(z * cy, cy), cy)]
        zm2 = f[pl.ds(pl.multiple_of(lax.rem(z + nz - 2, nz) * cy, cy), cy)]
        zm1 = f[pl.ds(pl.multiple_of(lax.rem(z + nz - 1, nz) * cy, cy), cy)]
        zp1 = f[pl.ds(pl.multiple_of(lax.rem(z + 1, nz) * cy, cy), cy)]
        zp2 = f[pl.ds(pl.multiple_of(lax.rem(z + 2, nz) * cy, cy), cy)]
        ring[0:cy] = c
        ring[cy:cy + 1] = yg[0, pl.ds(z, 1)]
        ring[cy + 1:cy + 2] = yg[1, pl.ds(z, 1)]
        ring[cy + 6:cy + 7] = yg[2, pl.ds(z, 1)]
        ring[cy + 7:cy + 8] = yg[3, pl.ds(z, 1)]
        ry = ring[...]
        ym2 = pltpu.roll(ry, 2, 0)[:cy]
        ym1 = pltpu.roll(ry, 1, 0)[:cy]
        yp1 = pltpu.roll(ry, cy + 7, 0)[:cy]
        yp2 = pltpu.roll(ry, cy + 6, 0)[:cy]
        rx = jnp.concatenate([c, xe[pl.ds(pl.multiple_of(z * cy, cy), cy)]], axis=1)
        wide = cx + 128
        xm2 = pltpu.roll(rx, 2, 1)[:, :cx]
        xm1 = pltpu.roll(rx, 1, 1)[:, :cx]
        xp1 = pltpu.roll(rx, wide - 1, 1)[:, :cx]
        xp2 = pltpu.roll(rx, wide - 2, 1)[:, :cx]
        u = vel[0, z].astype(jnp.float32) + mean_flow
        v = vel[1, z].astype(jnp.float32)
        w = vel[2, z].astype(jnp.float32)
        gx_ = c8 * (xp1 - xm1) - c1 * (xp2 - xm2)
        gy_ = c8 * (yp1 - ym1) - c1 * (yp2 - ym2)
        gz_ = c8 * (zp1 - zm1) - c1 * (zp2 - zm2)
        near = ((xp1 + xm1) + (yp1 + ym1)) + (zp1 + zm1)
        far = ((xp2 + xm2) + (yp2 + ym2)) + (zp2 + zm2)
        rhs = (d16 * near - d1 * far - d30 * c) - u * gx_ - v * (gy_ + mean_gradient) - w * gz_
        euler = c + time_step * rhs
        store(z, pl.ds(pl.multiple_of(z * cy, cy), cy), euler)
        return carry

    lax.fori_loop(0, nz, plane, 0, unroll=2)


def particles(second, rows, rt, now, nxt, field, accs, buf, peers):
    cx = field.shape[1]
    cap = buf.shape[1]
    scale = time_step * heat_share * (0.25 if second else 1.0)
    lane = lax.broadcasted_iota(jnp.int32, (cap, cx), 1)
    src = lax.broadcasted_iota(jnp.int32, (cap, LANES), 1)

    def group(b, carry):
        s = b * GROUP
        turn = lax.rem(LANES - s, LANES)
        t = pltpu.roll(rt[...], turn, 1)
        old = pltpu.roll(now[...], turn, 1)
        made = nxt[...]
        for g in range(GROUP):
            for i in range(cap):
                buf[g, i:i + 1] = field[pl.ds(rows[s + g, i], 1)]
        for g in range(GROUP):
            hit = lane == t[0:cap, g:g + 1].astype(jnp.int32) % cx
            sample = jnp.sum(jnp.where(hit, buf[g], 0.0), axis=1, keepdims=True)
            temp = old[:, g:g + 1]
            flux = t[2 * cap:3 * cap, g:g + 1] * (temp - sample)
            new = temp + time_step * (t[3 * cap:, g:g + 1] - flux)
            if second:
                new = 0.75 * t[cap:2 * cap, g:g + 1] + 0.25 * new
            made = jnp.where(src == s + g, new, made)
            buf[g] = jnp.where(hit, scale * flux, 0.0)
        nxt[...] = made
        for g in range(GROUP):
            for i in range(0, cap, WAYS):
                ats = [pl.ds(rows[s + g, i + k], 1) for k in range(WAYS)]
                adds = [accs[k][ats[k]] + buf[g, i + k:i + k + 1] for k in range(WAYS)]
                for k in range(WAYS):
                    accs[k][ats[k]] = adds[k]
        return carry

    lax.fori_loop(0, peers // GROUP, group, 0)


def first_kernel(dims, full_y, f, vel, o_left, o_right, y_up, y_low, came, info, rows,
                 s1, q2, e_right, e_left, lo, hi, home,
                 xe, yg, ring, rt, t1, t2, buf, acc1, acc2, acc3):
    nz, cy, cx = dims
    peers = came.shape[0]
    cap = home.shape[2]
    zero = jnp.zeros((cy, cx), jnp.float32)

    def store(z, at, euler):
        s1[at] = euler
        for acc in (q2, acc1, acc2, acc3):
            acc[at] = zero

    stencil(dims, full_y, f, vel, o_left, o_right, y_up, y_low, info, xe, yg, ring, store)
    for half in range(2):
        got = came[:, half, :]
        if peers < LANES:
            got = jnp.concatenate([got, jnp.zeros((LANES - peers, 2 * cap), jnp.float32)], axis=0)
        rt[2 * cap * half:2 * cap * (half + 1)] = got.T
    t1[...] = jnp.zeros_like(t1)
    t2[...] = jnp.zeros_like(t2)
    particles(False, rows, rt, rt.at[cap:2 * cap], t1, f, (s1, acc1, acc2, acc3), buf, peers)

    def total_one(i, carry):
        at = pl.ds(pl.multiple_of(i * 128, 128), 128)
        new = (s1[at] + acc1[at]) + (acc2[at] + acc3[at])
        s1[at] = new
        for acc in (acc1, acc2, acc3):
            acc[at] = jnp.zeros_like(new)
        put_ends(new, i, dims, e_right, e_left, lo, hi)
        return carry

    lax.fori_loop(0, nz * cy // 128, total_one, 0)
    particles(True, rows, rt, t1, t2, s1, (q2, acc1, acc2, acc3), buf, peers)
    home[:, 0, :] = t2[...].T[:peers]

    def total_two(i, carry):
        at = pl.ds(pl.multiple_of(i * 64, 64), 64)
        q2[at] = (q2[at] + acc1[at]) + (acc2[at] + acc3[at])
        return carry

    lax.fori_loop(0, nz * cy // 64, total_two, 0)


def work_space(dims):
    nz, cy, cx = dims
    f32 = jnp.float32
    return [pltpu.VMEM((nz * cy, 128), f32), pltpu.VMEM((4, nz, cx), f32), pltpu.VMEM((cy + 8, cx), f32)]


def first(dims, full_y, cap, f, vel, halos, came, info, rows):
    nz, cy, cx = dims
    f32 = jnp.float32
    vm = pl.BlockSpec(memory_space=pltpu.VMEM)
    sm = pl.BlockSpec(memory_space=pltpu.SMEM)
    grid = jax.ShapeDtypeStruct((nz * cy, cx), f32)
    space = pltpu.VMEM((nz * cy, cx), f32)
    return pl.pallas_call(
        functools.partial(first_kernel, dims, full_y),
        out_shape=[grid, grid] + ends_shapes(dims) + [jax.ShapeDtypeStruct((came.shape[0], 1, cap), f32)],
        in_specs=[vm] * 7 + [sm, sm],
        out_specs=[vm] * 7,
        scratch_shapes=work_space(dims) + [
            pltpu.VMEM((4 * cap, LANES), f32), pltpu.VMEM((cap, LANES), f32), pltpu.VMEM((cap, LANES), f32),
            pltpu.VMEM((GROUP, cap, cx), f32), space, space, space],
        compiler_params=pltpu.CompilerParams(vmem_limit_bytes=26 * MIB),
        name="section_one",
    )(f, vel, *halos, came, info, rows)


def second_kernel(dims, full_y, f, vel, o_left, o_right, y_up, y_low, f0, q2, home, count, info,
                  out, temp_out, xe, yg, ring):
    def store(z, at, euler):
        out[z] = 0.75 * f0[at] + 0.25 * euler + q2[at]

    back = home[:, 0, :]
    slot = lax.broadcasted_iota(jnp.int32, back.shape, 1)
    temp_out[0] = jnp.where(slot < column(count[...]), back, 0.0)
    stencil(dims, full_y, f, vel, o_left, o_right, y_up, y_low, info, xe, yg, ring, store)


def second(dims, full_y, f, vel, halos, f0, q2, home, count, info):
    f32 = jnp.float32
    vm = pl.BlockSpec(memory_space=pltpu.VMEM)
    return pl.pallas_call(
        functools.partial(second_kernel, dims, full_y),
        out_shape=[jax.ShapeDtypeStruct(dims, f32),
                   jax.ShapeDtypeStruct((1, home.shape[0], home.shape[2]), f32)],
        in_specs=[vm] * 10 + [pl.BlockSpec(memory_space=pltpu.SMEM)],
        out_specs=[vm] * 2,
        scratch_shapes=work_space(dims),
        compiler_params=pltpu.CompilerParams(vmem_limit_bytes=26 * MIB),
        name="section_two",
    )(f, vel, *halos, f0, q2, home, count, info)


def on_device(
    scalar_field, velocity, shear_offset, part_temp, part_coef, part_heat, part_cell, part_count
):
    nz, cy, cx = scalar_field.shape
    cap = part_temp.shape[2]
    gx_index = lax.axis_index("gx")
    gy_index = lax.axis_index("gy")
    gx_count = lax.axis_size("gx")
    gy_count = lax.axis_size("gy")
    full_x = cx * gx_count
    full_y = cy * gy_count
    dims = (nz, cy, cx)
    field = scalar_field.reshape(nz * cy, cx)

    def info(offset):
        low_shift = jnp.where(gy_index == 0, (full_x - offset) % full_x, 0)
        high_shift = jnp.where(gy_index == gy_count - 1, offset, 0)
        up = (gx_index * cx - high_shift) % full_x
        low = (gx_index * cx - low_shift) % full_x
        return jnp.stack([up // cx, up % cx, low // cx, low % cx, gy_index]).astype(jnp.int32)

    sends = prepare(dims, field, part_cell, part_temp, part_coef, part_heat, part_count)
    *halos, came = exchange(0, gx_count, gy_count, *sends)
    rows = came[:, 0, :cap].astype(jnp.int32) // cx
    section_one, source, *sends = first(
        dims, full_y, cap, field, velocity, halos, came, info(shear_offset[0]), rows)
    *halos, home = exchange(1, gx_count, gy_count, *sends)
    scalar_out, temp_out = second(
        dims, full_y, section_one, velocity, halos, field, source, home, part_count,
        info(shear_offset[1]))
    return (scalar_out, temp_out)


def solution(mesh):
    in_specs = (
        P(None, "gy", "gx"),
        P(None, None, "gy", "gx"),
        P(),
        P(("gx", "gy"), None, None),
        P(("gx", "gy"), None, None),
        P(("gx", "gy"), None, None),
        P(("gx", "gy"), None, None),
        P(("gx", "gy"), None),
    )
    out_specs = (P(None, "gy", "gx"), P(("gx", "gy"), None, None))
    return jax.shard_map(
        on_device, mesh=mesh, in_specs=in_specs, out_specs=out_specs, check_vma=False
    )
```

time: 126 us -> 89.3 us (0.71); the launches traced: 124 us -> 88.8 us
  local copies, waits for them, and re-layouts: 30.2 us -> 8.5 us
  starting transfers between devices: 13.7 us -> 0 us
  Pallas kernels: 73.1 us -> 76.8 us
  other arithmetic: 3.2 us -> 0.02 us
    all_to_all x2 -> x0, starting transfers between devices: 13.7 us -> none  [the longest x1 7.3 us: on_device(): came = lax.all_to_all(send, both, split_axis=0, concat_axis=0, tiled=True)]
    unnamed x46 -> x20, local copies, waits for them, and re-layouts: 19.6 us -> 7.01 us
    slice x6 -> x0, local copies, waits for them, and re-layouts: 4.38 us -> none  [the longest x1 2.88 us: ends(): return field[:, :, at:at + 2].reshape(nz * cy, 2).T]
    pallas_call x6 -> x5, Pallas kernels: 73.1 us -> 76.8 us  [the longest x2 33.3 us: exchange(): pl.pallas_call(functools.partial(exchange_kernel, gx_count, gy_count), ou...]
    reshape x4 -> x0, local copies, waits for them, and re-layouts: 3.18 us -> none  [the longest x2 3.08 us: ends(): return field[:, :, at:at + 2].reshape(nz * cy, 2).T]
    squeeze x2 -> x0, other arithmetic: 1.51 us -> none  [the longest x1 0.79 us: on_device(): live_coef[0]]
    all_to_all x2 -> x0, local copies, waits for them, and re-layouts: 1.32 us -> none  [the longest x1 0.68 us: on_device(): lax.all_to_all(pack[4].reshape(peers, cap), both, split_axis=0, concat_ax...]
  transfers between devices with their start and end apart: 2 -> 0, of which waited for: 0 -> 0; matrix products, arithmetic and copies ran while one was open for 7% -> 0% of each run, Pallas kernels for 34% -> 0%
where the time goes in v2:
time: 89.3 us; the launch traced here: 88.8 us
  Pallas kernels  76.8 us (86%)
  local copies, waits for them, and re-layouts  8.5 us (10%)
  between operations  3.5 us (4%)
    pallas_call x2, Pallas kernels, exchange(): pl.pallas_call(functools.partial(exchange_kernel, gx_count, gy_count), ou...  33.3 us
    pallas_call x1, Pallas kernels, first(): pl.pallas_call(functools.partial(first_kernel, dims, full_y), out_shape=[...  31.5 us
    pallas_call x1, Pallas kernels, second(): pl.pallas_call(functools.partial(second_kernel, dims, full_y), out_shape=...  9.6 us
    unnamed x20, local copies, waits for them, and re-layouts  7.01 us
    pallas_call x1, Pallas kernels, prepare(): pl.pallas_call(functools.partial(prepare_kernel, dims), out_shape=ends_sh...  2.36 us

profile of v2, /device:TPU:0, one launch (start us, length us, event | category | flops | bytes accessed | tf_op | source)
XLA Modules:
  0.0 88.8 jit_solution(11540322755543660417)
XLA Ops:
  0.6 1.3 %fusion.3 = (s32[1]{0:T(128)}, s32[1]{0:T(128)}) fusion(s32[2]{0:T(128)} %param.10), kind=kLoop, calls=%fused_computation.9 | loop fusion | bytes 16 | tf_op jit(solution)/shard_map/slice | solution.py:453
  4.7 0.1 stack.44.info
  4.8 0.1 stack.39.info
  4.9 0.0 copy-start
  4.9 1.6 %copy-done = f32[64,32,256]{2,1,0:T(8,128)S(1)} copy-done((f32[64,32,256]{2,1,0:T(8,128)S(1)}, f32[64,32,256]{2,1,0:T(8,128)}, u32[]{:S(2)}) %copy-start) | copy-done | bytes 2097176
  6.5 0.0 copy-start.4
  6.5 0.7 copy-done.4
  7.2 0.0 copy-start.5
  7.2 0.7 copy-done.5
  7.9 0.0 copy-start.6
  7.9 0.7 copy-done.6
  8.7 0.0 copy-start.7
  8.7 0.7 copy-done.7
  9.4 0.0 copy-start.8
  9.4 0.7 copy-done.8
  10.0 0.0 copy-start.1
  10.0 2.4 %prepare.1 = (f32[2,2048]{1,0:T(2,128)S(1)}, f32[2,2048]{1,0:T(2,128)S(1)}, f32[2,64,256]{2,1,0:T(8,128)S(1)}, f32[2,64,256]{2,1,0:T(8,128)S(1)}, f32[32,2,128]{2,1,0:T(2,128)S(1)}) custom-call(f32[2048,256]{1,0:T(8,128)S(1)} %bitcast.16, s32[1,32,64]{2,1,0:T(8,128)S(1)} %copy-done.4, f32[1,32,64]{2,1,0:T(8,128)S(1)} %copy-done.5, ...), custom_call_target="tpu_custom_call" | custom-call | tf_op jit(solution)/shard_map/prepare/pallas_call | solution.py:209
  12.4 17.5 %exchange_0.1 = (f32[2,2048]{1,0:T(2,128)S(1)}, f32[2,2048]{1,0:T(2,128)S(1)}, f32[4,2,64,256]{3,2,1,0:T(8,128)S(1)}, f32[4,2,64,256]{3,2,1,0:T(8,128)S(1)}, f32[32,2,128]{2,1,0:T(2,128)S(1)}) custom-call(f32[2,2048]{1,0:T(2,128)S(1)} %get-tuple-element.24.e_right, f32[2,2048]{1,0:T(2,128)S(1)} %get-tuple-element.25.e_left, ...), custom_call_target="tpu_custom_call" | custom-call | tf_op jit(solution)/shard_map/exchange_0/pallas_call | solution.py:149
  30.0 0.0 copy-done.1
  30.0 0.0 copy-start.2
  30.0 1.9 %copy-done.2 = bf16[3,64,32,256]{3,2,1,0:T(8,128)(2,1)S(1)} copy-done((bf16[3,64,32,256]{3,2,1,0:T(8,128)(2,1)S(1)}, bf16[3,64,32,256]{3,2,1,0:T(8,128)(2,1)}, u32[]{:S(2)}) %copy-start.2) | copy-done | bytes 3145752
  31.9 0.0 copy-start.3
  31.9 0.0 copy-start.9
  31.9 31.5 %section_one.1 = (f32[2048,256]{1,0:T(8,128)S(1)}, f32[2048,256]{1,0:T(8,128)S(1)}, f32[2,2048]{1,0:T(2,128)S(1)}, f32[2,2048]{1,0:T(2,128)S(1)}, f32[2,64,256]{...) custom-call(f32[2048,256]{1,0:T(8,128)S(1)} %bitcast.17, bf16[3,64,32,256]{3,2,1,0:T(8,128)(2,1)S(1)} %copy-done.2, ...), custom_call_target="tpu_custom_call" | custom-call | tf_op jit(solution)/shard_map/section_one/pallas_call | solution.py:385
  63.3 15.8 %exchange_1.1 = (f32[2,2048]{1,0:T(2,128)S(1)}, f32[2,2048]{1,0:T(2,128)S(1)}, f32[4,2,64,256]{3,2,1,0:T(8,128)S(1)}, f32[4,2,64,256]{3,2,1,0:T(8,128)S(1)}, f32[32,1,64]{2,1,0:T(1,128)S(1)}) custom-call(f32[2,2048]{1,0:T(2,128)S(1)} %get-tuple-element.35.e_right, f32[2,2048]{1,0:T(2,128)S(1)} %get-tuple-element.36.e_left, ...), custom_call_target="tpu_custom_call" | custom-call | tf_op jit(solution)/shard_map/exchange_1/pallas_call | solution.py:149
  79.2 0.0 copy-done.3
  79.2 0.0 copy-done.9
  79.2 9.6 %section_two.1 = (f32[64,32,256]{2,1,0:T(8,128)}, f32[1,32,64]{2,1,0:T(8,128)}) custom-call(f32[2048,256]{1,0:T(8,128)S(1)} %get-tuple-element.34.f, bf16[3,64,32,256]{3,2,1,0:T(8,128)(2,1)S(1)} %copy-done.3, f32[2,2048]{1,0:T(2,128)S(1)} %get-tuple-element.40.o_left, f32[2,2048]{1,0:T(2,128)S(1)} %get-tuple-element.41.o_right, ...), custom_call_target="tpu_custom_call" | custom-call | tf_op jit(solution)/shard_map/section_two/pallas_call | solution.py:412
  (2 shorter events, 0.0 us)
Async XLA Ops:
  4.9 1.6 %copy-start = (f32[64,32,256]{2,1,0:T(8,128)S(1)}, f32[64,32,256]{2,1,0:T(8,128)}, u32[]{:S(2)}) copy-start(f32[64,32,256]{2,1,0:T(8,128)} %param.8) | copy-start | bytes 6291460
  6.5 0.7 copy-start.4
  7.2 0.7 copy-start.5
  7.9 0.7 copy-start.6
  8.7 0.7 copy-start.7
  9.4 0.7 copy-start.8
  10.0 19.9 %copy-start.1 = (f32[64,32,256]{2,1,0:T(8,128)S(1)}, f32[64,32,256]{2,1,0:T(8,128)}, u32[]{:S(2)}) copy-start(f32[64,32,256]{2,1,0:T(8,128)} %param.8) | copy-start | bytes 6291460
  30.0 1.9 %copy-start.2 = (bf16[3,64,32,256]{3,2,1,0:T(8,128)(2,1)S(1)}, bf16[3,64,32,256]{3,2,1,0:T(8,128)(2,1)}, u32[]{:S(2)}) copy-start(bf16[3,64,32,256]{3,2,1,0:T(8,128)(2,1)} %vel.3) | copy-start | bytes 9437188
  31.9 47.3 %copy-start.3 = (bf16[3,64,32,256]{3,2,1,0:T(8,128)(2,1)S(1)}, bf16[3,64,32,256]{3,2,1,0:T(8,128)(2,1)}, u32[]{:S(2)}) copy-start(bf16[3,64,32,256]{3,2,1,0:T(8,128)(2,1)} %vel.3) | copy-start | bytes 9437188
  31.9 47.3 %copy-start.9 = (s32[1,32]{1,0:T(1,128)S(1)}, s32[1,32]{1,0:T(1,128)}, u32[]{:S(2)}) copy-start(s32[1,32]{1,0:T(1,128)} %count.3) | copy-start | bytes 388

commit v3 on v2

--- a/solution.py
+++ b/solution.py
@@ -15,13 +15,20 @@
 
 MESH = pl.DeviceIdType.MESH
 MIB = 1 << 20
-GROUP = 4
+GROUP = 8
 LANES = 128
 WAYS = 4
 
 
-def exchange_kernel(gx_count, gy_count, e_right, e_left, lo, hi, mail, o_left, o_right, y_up, y_low, came,
-                    send_x, recv_x, send_lo, recv_up, send_hi, recv_low, send_p, recv_p, own_sem):
+def exchange_kernel(gx_count, gy_count, loads, *refs):
+    if loads:
+        e_right, e_left, lo, hi, mail, held, o_left, o_right, y_up, y_low, came, near = refs[:12]
+        send_x, recv_x, send_lo, recv_up, send_hi, recv_low, send_p, recv_p, own_sem, load_sem = refs[12:]
+        vel = (held, near, load_sem)
+    else:
+        e_right, e_left, lo, hi, mail, o_left, o_right, y_up, y_low, came = refs[:10]
+        send_x, recv_x, send_lo, recv_up, send_hi, recv_low, send_p, recv_p, own_sem = refs[10:]
+        vel = None
     gx = lax.axis_index("gx")
     gy = lax.axis_index("gy")
     right = lax.rem(gx + 1, gx_count)
@@ -31,27 +38,19 @@
 
     barrier = pltpu.get_barrier_semaphore()
 
-    peers = gx_count * gy_count
     me = gx * gy_count + gy
-
-    def peer(i):
-        d = lax.rem(me + i, peers)
-        return d, (d // gy_count, lax.rem(d, gy_count))
-
-    def greet(i, carry):
-        pl.semaphore_signal(barrier, inc=1, device_id=peer(i)[1], device_id_type=MESH)
-        return carry
-
-    lax.fori_loop(1, peers, greet, 0)
+    xs = [gx] + [lax.rem(gx + i, gx_count) for i in range(1, gx_count)]
+    ys = [gy] + [lax.rem(gy + i, gy_count) for i in range(1, gy_count)]
+    others = [(x * gy_count + y, (x, y)) for y in ys for x in xs][1:]
+    for _, place in others:
+        pl.semaphore_signal(barrier, inc=1, device_id=place, device_id_type=MESH)
     own = pltpu.make_async_copy(mail.at[me], came.at[me], own_sem)
     own.start()
-    pl.semaphore_wait(barrier, peers - 1)
-
-    def copy_mail(i):
-        d, place = peer(i)
-        return pltpu.make_async_remote_copy(
-            src_ref=mail.at[d], dst_ref=came.at[me], send_sem=send_p.at[d], recv_sem=recv_p.at[me],
-            device_id=place, device_id_type=MESH)
+    load = None
+    if vel is not None:
+        load = pltpu.make_async_copy(vel[0], vel[1], vel[2])
+        load.start()
+    pl.semaphore_wait(barrier, len(others))
 
     def copy_x(src, dst, k, x):
         return pltpu.make_async_remote_copy(
@@ -93,11 +92,10 @@
     to_right.start()
     to_left.start()
 
-    def post(i, carry):
-        copy_mail(i).start()
-        return carry
-
-    lax.fori_loop(1, peers, post, 0)
+    for d, place in others:
+        pltpu.make_async_remote_copy(
+            src_ref=mail.at[d], dst_ref=came.at[me], send_sem=send_p.at[d], recv_sem=recv_p.at[me],
+            device_id=place, device_id_type=MESH).start()
 
     def arrive(rows, slots, sems, s):
         pltpu.make_async_remote_copy(
@@ -128,40 +126,38 @@
     to_right.wait_send()
     to_left.wait_send()
 
-    def finish(i, carry):
-        d, place = peer(i)
+    for d, place in others:
         copy = pltpu.make_async_remote_copy(
             src_ref=mail.at[d], dst_ref=came.at[d], send_sem=send_p.at[d], recv_sem=recv_p.at[d],
             device_id=place, device_id_type=MESH)
         copy.wait_recv()
         copy.wait_send()
-        return carry
-
-    lax.fori_loop(1, peers, finish, 0)
     own.wait()
-
-
-def exchange(which, gx_count, gy_count, e_right, e_left, lo, hi, mail):
+    if load is not None:
+        load.wait()
+
+
+def exchange(which, gx_count, gy_count, e_right, e_left, lo, hi, mail, *held):
     vm = pl.BlockSpec(memory_space=pltpu.VMEM)
     sem = pltpu.SemaphoreType.DMA
     f32 = jnp.float32
     peers = gx_count * gy_count
     return pl.pallas_call(
-        functools.partial(exchange_kernel, gx_count, gy_count),
+        functools.partial(exchange_kernel, gx_count, gy_count, bool(held)),
         out_shape=[
             jax.ShapeDtypeStruct(e_right.shape, f32),
             jax.ShapeDtypeStruct(e_left.shape, f32),
             jax.ShapeDtypeStruct((gx_count,) + lo.shape, f32),
             jax.ShapeDtypeStruct((gx_count,) + hi.shape, f32),
             jax.ShapeDtypeStruct(mail.shape, f32),
-        ],
-        in_specs=[vm] * 5,
-        out_specs=[vm] * 5,
-        scratch_shapes=[sem((2,)), sem((2,))] + [sem((gx_count,))] * 4 + [sem((peers,)), sem((peers,)), sem],
+        ] + [jax.ShapeDtypeStruct(h.shape, h.dtype) for h in held],
+        in_specs=[vm] * 5 + [pl.BlockSpec(memory_space=pltpu.HBM)] * len(held),
+        out_specs=[vm] * (5 + len(held)),
+        scratch_shapes=[sem((2,)), sem((2,))] + [sem((gx_count,))] * 4 + [sem((peers,)), sem((peers,)), sem] + [sem] * len(held),
         compiler_params=pltpu.CompilerParams(
             collective_id=which, has_side_effects=True, vmem_limit_bytes=8 * MIB),
         name="exchange_%d" % which,
-    )(e_right, e_left, lo, hi, mail)
+    )(e_right, e_left, lo, hi, mail, *held)
 
 
 def column(count):
@@ -183,12 +179,21 @@
             hi[row, pl.ds(z, 1)] = new[k * cy + cy - 2 + row:k * cy + cy - 1 + row]
 
 
-def prepare_kernel(dims, f, cell, temp, coef, heat, count, e_right, e_left, lo, hi, mail):
-    nz, cy, cx = dims
+def prepare_kernel(dims, f_at, cell_at, temp_at, coef_at, heat_at, count_at,
+                   e_right, e_left, lo, hi, mail, f, cell, temp, coef, heat, count, sems):
+    nz, cy, cx = dims
+    pairs = ((cell_at, cell), (temp_at, temp), (coef_at, coef), (heat_at, heat), (count_at, count), (f_at, f))
+    copies = [pltpu.make_async_copy(a, b, sems.at[k]) for k, (a, b) in enumerate(pairs)]
+    for c in copies:
+        c.start()
+    for c in copies[:-1]:
+        c.wait()
     slot = lax.broadcasted_iota(jnp.int32, coef.shape[1:], 1)
     live = jnp.where(slot < column(count[...]), coef[0], 0.0)
     mail[:, 0, :] = jnp.concatenate([cell[0].astype(jnp.float32), temp[0]], axis=1)
     mail[:, 1, :] = jnp.concatenate([live, heat[0]], axis=1)
+
+    copies[-1].wait()
 
     def part(i, carry):
         put_ends(f[pl.ds(pl.multiple_of(i * 128, 128), 128)], i, dims, e_right, e_left, lo, hi)
@@ -208,12 +213,27 @@
     peers, cap = cell.shape[1:]
     return pl.pallas_call(
         functools.partial(prepare_kernel, dims),
-        out_shape=ends_shapes(dims) + [jax.ShapeDtypeStruct((peers, 2, 2 * cap), jnp.float32)],
-        in_specs=[vm] * 6,
-        out_specs=[vm] * 5,
+        out_shape=ends_shapes(dims) + [
+            jax.ShapeDtypeStruct((peers, 2, 2 * cap), jnp.float32),
+            jax.ShapeDtypeStruct(f.shape, f.dtype)],
+        in_specs=[pl.BlockSpec(memory_space=pltpu.HBM)] * 6,
+        out_specs=[vm] * 6,
+        scratch_shapes=[pltpu.VMEM(a.shape, a.dtype) for a in (cell, temp, coef, heat, count)]
+        + [pltpu.SemaphoreType.DMA((6,))],
         compiler_params=pltpu.CompilerParams(vmem_limit_bytes=8 * MIB),
         name="prepare",
     )(f, cell, temp, coef, heat, count)
+
+
+def plan(which, dims, shear, gx_count, gy_count):
+    cx = dims[2]
+    gx = lax.axis_index("gx")
+    gy = lax.axis_index("gy")
+    full_x = cx * gx_count
+    offset = shear[which]
+    up = lax.rem(gx * cx + full_x - jnp.where(gy == gy_count - 1, offset, 0), full_x)
+    low = lax.rem(gx * cx + jnp.where(gy == 0, offset, 0), full_x)
+    return lax.div(up, cx), lax.rem(up, cx), lax.div(low, cx), lax.rem(low, cx), gy
 
 
 def stencil(dims, full_y, f, vel, o_left, o_right, y_up, y_low, info, xe, yg, ring, store):
@@ -325,13 +345,14 @@
     lax.fori_loop(0, peers // GROUP, group, 0)
 
 
-def first_kernel(dims, full_y, f, vel, o_left, o_right, y_up, y_low, came, info, rows,
+def first_kernel(dims, full_y, f, vel, o_left, o_right, y_up, y_low, came, shear, rows,
                  s1, q2, e_right, e_left, lo, hi, home,
                  xe, yg, ring, rt, t1, t2, buf, acc1, acc2, acc3):
     nz, cy, cx = dims
     peers = came.shape[0]
     cap = home.shape[2]
     zero = jnp.zeros((cy, cx), jnp.float32)
+    info = plan(0, dims, shear, y_up.shape[0], full_y // cy)
 
     def store(z, at, euler):
         s1[at] = euler
@@ -395,8 +416,10 @@
     )(f, vel, *halos, came, info, rows)
 
 
-def second_kernel(dims, full_y, f, vel, o_left, o_right, y_up, y_low, f0, q2, home, count, info,
+def second_kernel(dims, full_y, f, vel, o_left, o_right, y_up, y_low, f0, q2, home, count, shear,
                   out, temp_out, xe, yg, ring):
+    info = plan(1, dims, shear, y_up.shape[0], full_y // dims[1])
+
     def store(z, at, euler):
         out[z] = 0.75 * f0[at] + 0.25 * euler + q2[at]
 
@@ -426,31 +449,21 @@
 ):
     nz, cy, cx = scalar_field.shape
     cap = part_temp.shape[2]
-    gx_index = lax.axis_index("gx")
-    gy_index = lax.axis_index("gy")
     gx_count = lax.axis_size("gx")
     gy_count = lax.axis_size("gy")
-    full_x = cx * gx_count
     full_y = cy * gy_count
     dims = (nz, cy, cx)
     field = scalar_field.reshape(nz * cy, cx)
 
-    def info(offset):
-        low_shift = jnp.where(gy_index == 0, (full_x - offset) % full_x, 0)
-        high_shift = jnp.where(gy_index == gy_count - 1, offset, 0)
-        up = (gx_index * cx - high_shift) % full_x
-        low = (gx_index * cx - low_shift) % full_x
-        return jnp.stack([up // cx, up % cx, low // cx, low % cx, gy_index]).astype(jnp.int32)
-
-    sends = prepare(dims, field, part_cell, part_temp, part_coef, part_heat, part_count)
-    *halos, came = exchange(0, gx_count, gy_count, *sends)
+    *sends, near_field = prepare(dims, field, part_cell, part_temp, part_coef, part_heat, part_count)
+    *halos, came, near = exchange(0, gx_count, gy_count, *sends, velocity)
     rows = came[:, 0, :cap].astype(jnp.int32) // cx
     section_one, source, *sends = first(
-        dims, full_y, cap, field, velocity, halos, came, info(shear_offset[0]), rows)
+        dims, full_y, cap, near_field, near, halos, came, shear_offset, rows)
     *halos, home = exchange(1, gx_count, gy_count, *sends)
     scalar_out, temp_out = second(
-        dims, full_y, section_one, velocity, halos, field, source, home, part_count,
-        info(shear_offset[1]))
+        dims, full_y, section_one, near, halos, near_field, source, home, part_count,
+        shear_offset)
     return (scalar_out, temp_out)
 
 

time: 89.3 us -> 84.5 us (0.946)
  between operations: 3.5 us -> 0.73 us
  local copies, waits for them, and re-layouts: 8.5 us -> 7.01 us
    slice x1 -> x0, local copies, waits for them, and re-layouts: 1.31 us -> none  [on_device(): shear_offset[1]]
    unnamed x20 -> x18, local copies, waits for them, and re-layouts: 7.01 us -> 7.01 us
where the time goes in v3:
time: 84.5 us; the launch traced here: 84 us
  Pallas kernels  76.3 us (90%)
  local copies, waits for them, and re-layouts  7.01 us (8%)
    pallas_call x2, Pallas kernels, exchange(): pl.pallas_call(functools.partial(exchange_kernel, gx_count, gy_count, boo...  32.5 us
    pallas_call x1, Pallas kernels, first(): pl.pallas_call(functools.partial(first_kernel, dims, full_y), out_shape=[...  31.5 us
    pallas_call x1, Pallas kernels, second(): pl.pallas_call(functools.partial(second_kernel, dims, full_y), out_shape=...  9.63 us
    unnamed x18, local copies, waits for them, and re-layouts  7.01 us
    pallas_call x1, Pallas kernels, prepare(): pl.pallas_call(functools.partial(prepare_kernel, dims), out_shape=ends_sh...  2.64 us

profile of v3, /device:TPU:0, one launch (start us, length us, event | category | flops | bytes accessed | tf_op | source)
XLA Modules:
  0.0 84.0 jit_solution(15273759482352716500)
XLA Ops:
  0.6 0.0 copy-start.1
  0.6 1.6 %copy-done.1 = f32[64,32,256]{2,1,0:T(8,128)S(1)} copy-done((f32[64,32,256]{2,1,0:T(8,128)S(1)}, f32[64,32,256]{2,1,0:T(8,128)}, u32[]{:S(2)}) %copy-start.1) | copy-done | bytes 2097176
  2.2 0.0 copy-start.2
  2.2 0.7 copy-done.2
  2.9 0.0 copy-start.3
  2.9 0.7 copy-done.3
  3.7 0.0 copy-start.4
  3.7 0.7 copy-done.4
  4.4 0.0 copy-start.5
  4.4 0.7 copy-done.5
  5.1 0.0 copy-start.6
  5.1 0.7 copy-done.6
  5.8 2.6 %prepare.1 = (f32[2,2048]{1,0:T(2,128)S(1)}, f32[2,2048]{1,0:T(2,128)S(1)}, f32[2,64,256]{2,1,0:T(8,128)S(1)}, f32[2,64,256]{2,1,0:T(8,128)S(1)}, f32[32,2,128]{2,1,0:T(2,128)S(1)}, /*index=5*/f32[2048,256]{1,0:T(8,128)S(1)}) custom-call(f32[2048,256]{1,0:T(8,128)S(1)} %bitcast.5, s32[1,32,64]{2,1,0:T(8,128)S(1)} %copy-done.2, f32[1,32,64]{2,1,0:T(8,128)S(1)} %copy-done.3, ...), custom_call_target="tpu_custom_call" | custom-call | tf_op jit(solution)/shard_map/prepare/pallas_call | solution.py:214
  8.4 0.0 copy-start.8
  8.4 0.0 copy-start
  8.4 1.9 %copy-done = bf16[3,64,32,256]{3,2,1,0:T(8,128)(2,1)S(1)} copy-done((bf16[3,64,32,256]{3,2,1,0:T(8,128)(2,1)S(1)}, bf16[3,64,32,256]{3,2,1,0:T(8,128)(2,1)}, u32[]{:S(2)}) %copy-start) | copy-done | bytes 3145752
  10.3 17.2 %exchange_0.1 = (f32[2,2048]{1,0:T(2,128)S(1)}, f32[2,2048]{1,0:T(2,128)S(1)}, f32[4,2,64,256]{3,2,1,0:T(8,128)S(1)}, f32[4,2,64,256]{3,2,1,0:T(8,128)S(1)}, f32...) custom-call(f32[2,2048]{1,0:T(2,128)S(1)} %get-tuple-element.27.refs_0_, ...), custom_call_target="tpu_custom_call" | custom-call | tf_op jit(solution)/shard_map/exchange_0/pallas_call | solution.py:145
  27.5 0.0 copy-done.8
  27.5 0.0 copy-start.7
  27.5 31.5 %section_one.1 = (f32[2048,256]{1,0:T(8,128)S(1)}, f32[2048,256]{1,0:T(8,128)S(1)}, f32[2,2048]{1,0:T(2,128)S(1)}, f32[2,2048]{1,0:T(2,128)S(1)}, f32[2,64,256]{...) custom-call(f32[2048,256]{1,0:T(8,128)S(1)} %get-tuple-element.26.f.f0, ...), custom_call_target="tpu_custom_call" | custom-call | tf_op jit(solution)/shard_map/section_one/pallas_call | solution.py:406
  59.0 15.4 %exchange_1.1 = (f32[2,2048]{1,0:T(2,128)S(1)}, f32[2,2048]{1,0:T(2,128)S(1)}, f32[4,2,64,256]{3,2,1,0:T(8,128)S(1)}, f32[4,2,64,256]{3,2,1,0:T(8,128)S(1)}, f32[32,1,64]{2,1,0:T(1,128)S(1)}) custom-call(f32[2,2048]{1,0:T(2,128)S(1)} %get-tuple-element.39.refs_0_, f32[2,2048]{1,0:T(2,128)S(1)} %get-tuple-element.40.refs_1_, ...), custom_call_target="tpu_custom_call" | custom-call | tf_op jit(solution)/shard_map/exchange_1/pallas_call | solution.py:145
  74.4 0.0 copy-done.7
  74.4 9.6 %section_two.1 = (f32[64,32,256]{2,1,0:T(8,128)}, f32[1,32,64]{2,1,0:T(8,128)}) custom-call(f32[2048,256]{1,0:T(8,128)S(1)} %get-tuple-element.38.f, bf16[3,64,32,256]{3,2,1,0:T(8,128)(2,1)S(1)} %get-tuple-element.32.vel, f32[2,2048]{1,0:T(2,128)S(1)} %get-tuple-element.44.o_left, f32[2,2048]{1,0:T(2,128)S(1)} %get-tuple-element.45.o_right, ...), custom_call_target="tpu_custom_call" | custom-call | tf_op jit(solution)/shard_map/section_two/pallas_call | solution.py:435
  (2 shorter events, 0.0 us)
Async XLA Ops:
  0.6 1.6 %copy-start.1 = (f32[64,32,256]{2,1,0:T(8,128)S(1)}, f32[64,32,256]{2,1,0:T(8,128)}, u32[]{:S(2)}) copy-start(f32[64,32,256]{2,1,0:T(8,128)} %param.8) | copy-start | bytes 6291460
  2.2 0.7 copy-start.2
  2.9 0.7 copy-start.3
  3.7 0.7 copy-start.4
  4.4 0.7 copy-start.5
  5.1 0.7 copy-start.6
  8.4 19.1 %copy-start.8 = (s32[2]{0:T(128)S(1)}, s32[2]{0:T(128)}, u32[]{:S(2)}) copy-start(s32[2]{0:T(128)} %shear.3) | copy-start | bytes 28
  8.4 1.9 %copy-start = (bf16[3,64,32,256]{3,2,1,0:T(8,128)(2,1)S(1)}, bf16[3,64,32,256]{3,2,1,0:T(8,128)(2,1)}, u32[]{:S(2)}) copy-start(bf16[3,64,32,256]{3,2,1,0:T(8,128)(2,1)} %refs_5_.1) | copy-start | bytes 9437188
  27.5 46.9 %copy-start.7 = (s32[1,32]{1,0:T(1,128)S(1)}, s32[1,32]{1,0:T(1,128)}, u32[]{:S(2)}) copy-start(s32[1,32]{1,0:T(1,128)} %count.1) | copy-start | bytes 388

commit v4 on v3

--- a/solution.py
+++ b/solution.py
@@ -86,7 +86,6 @@
         def _():
             act(copy_hi(0, gx, gy + 1))
 
-    all_copies(lambda c: c.start())
     to_right = copy_x(e_right, o_left, 0, right)
     to_left = copy_x(e_left, o_right, 1, left)
     to_right.start()
@@ -96,6 +95,7 @@
         pltpu.make_async_remote_copy(
             src_ref=mail.at[d], dst_ref=came.at[me], send_sem=send_p.at[d], recv_sem=recv_p.at[me],
             device_id=place, device_id_type=MESH).start()
+    all_copies(lambda c: c.start())
 
     def arrive(rows, slots, sems, s):
         pltpu.make_async_remote_copy(
@@ -308,10 +308,9 @@
 
 
 def particles(second, rows, rt, now, nxt, field, accs, buf, peers):
-    cx = field.shape[1]
     cap = buf.shape[1]
     scale = time_step * heat_share * (0.25 if second else 1.0)
-    lane = lax.broadcasted_iota(jnp.int32, (cap, cx), 1)
+    lane = lax.broadcasted_iota(jnp.int32, (cap, LANES), 1)
     src = lax.broadcasted_iota(jnp.int32, (cap, LANES), 1)
 
     def group(b, carry):
@@ -324,7 +323,7 @@
             for i in range(cap):
                 buf[g, i:i + 1] = field[pl.ds(rows[s + g, i], 1)]
         for g in range(GROUP):
-            hit = lane == t[0:cap, g:g + 1].astype(jnp.int32) % cx
+            hit = lane == t[0:cap, g:g + 1].astype(jnp.int32) % LANES
             sample = jnp.sum(jnp.where(hit, buf[g], 0.0), axis=1, keepdims=True)
             temp = old[:, g:g + 1]
             flux = t[2 * cap:3 * cap, g:g + 1] * (temp - sample)
@@ -347,17 +346,22 @@
 
 def first_kernel(dims, full_y, f, vel, o_left, o_right, y_up, y_low, came, shear, rows,
                  s1, q2, e_right, e_left, lo, hi, home,
-                 xe, yg, ring, rt, t1, t2, buf, acc1, acc2, acc3):
+                 xe, yg, ring, rt, t1, t2, buf, split, *accs):
     nz, cy, cx = dims
     peers = came.shape[0]
     cap = home.shape[2]
-    zero = jnp.zeros((cy, cx), jnp.float32)
+    zero = jnp.zeros((cy, LANES), jnp.float32)
+    cells = nz * cy
+    halves = [(h * cells, slice(h * LANES, (h + 1) * LANES)) for h in range(cx // LANES)]
     info = plan(0, dims, shear, y_up.shape[0], full_y // cy)
 
     def store(z, at, euler):
-        s1[at] = euler
-        for acc in (q2, acc1, acc2, acc3):
-            acc[at] = zero
+        for base, half in halves:
+            to = pl.ds(pl.multiple_of(base + z * cy, cy), cy)
+            split[to] = f[at, half]
+            accs[0][to] = euler[:, half]
+            for acc in accs[1:]:
+                acc[to] = zero
 
     stencil(dims, full_y, f, vel, o_left, o_right, y_up, y_low, info, xe, yg, ring, store)
     for half in range(2):
@@ -367,24 +371,32 @@
         rt[2 * cap * half:2 * cap * (half + 1)] = got.T
     t1[...] = jnp.zeros_like(t1)
     t2[...] = jnp.zeros_like(t2)
-    particles(False, rows, rt, rt.at[cap:2 * cap], t1, f, (s1, acc1, acc2, acc3), buf, peers)
+    particles(False, rows, rt, rt.at[cap:2 * cap], t1, split, accs, buf, peers)
 
     def total_one(i, carry):
         at = pl.ds(pl.multiple_of(i * 128, 128), 128)
-        new = (s1[at] + acc1[at]) + (acc2[at] + acc3[at])
-        s1[at] = new
-        for acc in (acc1, acc2, acc3):
-            acc[at] = jnp.zeros_like(new)
+        news = []
+        for base, half in halves:
+            to = pl.ds(pl.multiple_of(base + i * 128, 128), 128)
+            new = (accs[0][to] + accs[1][to]) + (accs[2][to] + accs[3][to])
+            s1[at, half] = new
+            split[to] = new
+            for acc in accs:
+                acc[to] = jnp.zeros_like(new)
+            news.append(new)
+        new = jnp.concatenate(news, axis=1)
         put_ends(new, i, dims, e_right, e_left, lo, hi)
         return carry
 
     lax.fori_loop(0, nz * cy // 128, total_one, 0)
-    particles(True, rows, rt, t1, t2, s1, (q2, acc1, acc2, acc3), buf, peers)
+    particles(True, rows, rt, t1, t2, split, accs, buf, peers)
     home[:, 0, :] = t2[...].T[:peers]
 
     def total_two(i, carry):
         at = pl.ds(pl.multiple_of(i * 64, 64), 64)
-        q2[at] = (q2[at] + acc1[at]) + (acc2[at] + acc3[at])
+        for base, half in halves:
+            to = pl.ds(pl.multiple_of(base + i * 64, 64), 64)
+            q2[at, half] = (accs[0][to] + accs[1][to]) + (accs[2][to] + accs[3][to])
         return carry
 
     lax.fori_loop(0, nz * cy // 64, total_two, 0)
@@ -402,7 +414,7 @@
     vm = pl.BlockSpec(memory_space=pltpu.VMEM)
     sm = pl.BlockSpec(memory_space=pltpu.SMEM)
     grid = jax.ShapeDtypeStruct((nz * cy, cx), f32)
-    space = pltpu.VMEM((nz * cy, cx), f32)
+    space = pltpu.VMEM((nz * cy * (cx // LANES), LANES), f32)
     return pl.pallas_call(
         functools.partial(first_kernel, dims, full_y),
         out_shape=[grid, grid] + ends_shapes(dims) + [jax.ShapeDtypeStruct((came.shape[0], 1, cap), f32)],
@@ -410,7 +422,7 @@
         out_specs=[vm] * 7,
         scratch_shapes=work_space(dims) + [
             pltpu.VMEM((4 * cap, LANES), f32), pltpu.VMEM((cap, LANES), f32), pltpu.VMEM((cap, LANES), f32),
-            pltpu.VMEM((GROUP, cap, cx), f32), space, space, space],
+            pltpu.VMEM((GROUP, cap, LANES), f32)] + [space] * 5,
         compiler_params=pltpu.CompilerParams(vmem_limit_bytes=26 * MIB),
         name="section_one",
     )(f, vel, *halos, came, info, rows)
@@ -457,7 +469,8 @@
 
     *sends, near_field = prepare(dims, field, part_cell, part_temp, part_coef, part_heat, part_count)
     *halos, came, near = exchange(0, gx_count, gy_count, *sends, velocity)
-    rows = came[:, 0, :cap].astype(jnp.int32) // cx
+    cells = came[:, 0, :cap].astype(jnp.int32)
+    rows = cells % cx // LANES * (nz * cy) + cells // cx
     section_one, source, *sends = first(
         dims, full_y, cap, near_field, near, halos, came, shear_offset, rows)
     *halos, home = exchange(1, gx_count, gy_count, *sends)

time: 84.5 us -> 79.2 us (0.937)
  Pallas kernels: 76.3 us -> 70.1 us
    pallas_call x1, Pallas kernels: 31.5 us -> 27.1 us  [first(): pl.pallas_call(functools.partial(first_kernel, dims, full_y), out_shape=[...]
    pallas_call x2, Pallas kernels: 32.5 us -> 30.8 us  [exchange(): pl.pallas_call(functools.partial(exchange_kernel, gx_count, gy_count, boo...]
where the time goes in v4:
time: 79.2 us; the launch traced here: 77.9 us
  Pallas kernels  70.1 us (89%)
  local copies, waits for them, and re-layouts  7.01 us (9%)
    pallas_call x2, Pallas kernels, exchange(): pl.pallas_call(functools.partial(exchange_kernel, gx_count, gy_count, boo...  30.8 us
    pallas_call x1, Pallas kernels, first(): pl.pallas_call(functools.partial(first_kernel, dims, full_y), out_shape=[...  27.1 us
    pallas_call x1, Pallas kernels, second(): pl.pallas_call(functools.partial(second_kernel, dims, full_y), out_shape=...  9.63 us
    unnamed x18, local copies, waits for them, and re-layouts  7.01 us
    pallas_call x1, Pallas kernels, prepare(): pl.pallas_call(functools.partial(prepare_kernel, dims), out_shape=ends_sh...  2.64 us

profile of v4, /device:TPU:0, one launch (start us, length us, event | category | flops | bytes accessed | tf_op | source)
XLA Modules:
  0.0 77.9 jit_solution(5856882030897392122)
XLA Ops:
  0.6 0.0 copy-start.1
  0.6 1.6 %copy-done.1 = f32[64,32,256]{2,1,0:T(8,128)S(1)} copy-done((f32[64,32,256]{2,1,0:T(8,128)S(1)}, f32[64,32,256]{2,1,0:T(8,128)}, u32[]{:S(2)}) %copy-start.1) | copy-done | bytes 2097176
  2.2 0.0 copy-start.2
  2.2 0.7 copy-done.2
  2.9 0.0 copy-start.3
  2.9 0.7 copy-done.3
  3.7 0.0 copy-start.4
  3.7 0.7 copy-done.4
  4.4 0.0 copy-start.5
  4.4 0.7 copy-done.5
  5.1 0.0 copy-start.6
  5.1 0.7 copy-done.6
  5.8 2.6 %prepare.1 = (f32[2,2048]{1,0:T(2,128)S(1)}, f32[2,2048]{1,0:T(2,128)S(1)}, f32[2,64,256]{2,1,0:T(8,128)S(1)}, f32[2,64,256]{2,1,0:T(8,128)S(1)}, f32[32,2,128]{2,1,0:T(2,128)S(1)}, /*index=5*/f32[2048,256]{1,0:T(8,128)S(1)}) custom-call(f32[2048,256]{1,0:T(8,128)S(1)} %bitcast.5, s32[1,32,64]{2,1,0:T(8,128)S(1)} %copy-done.2, f32[1,32,64]{2,1,0:T(8,128)S(1)} %copy-done.3, ...), custom_call_target="tpu_custom_call" | custom-call | tf_op jit(solution)/shard_map/prepare/pallas_call | solution.py:214
  8.4 0.0 copy-start.8
  8.4 0.0 copy-start
  8.4 1.9 %copy-done = bf16[3,64,32,256]{3,2,1,0:T(8,128)(2,1)S(1)} copy-done((bf16[3,64,32,256]{3,2,1,0:T(8,128)(2,1)S(1)}, bf16[3,64,32,256]{3,2,1,0:T(8,128)(2,1)}, u32[]{:S(2)}) %copy-start) | copy-done | bytes 3145752
  10.3 15.9 %exchange_0.1 = (f32[2,2048]{1,0:T(2,128)S(1)}, f32[2,2048]{1,0:T(2,128)S(1)}, f32[4,2,64,256]{3,2,1,0:T(8,128)S(1)}, f32[4,2,64,256]{3,2,1,0:T(8,128)S(1)}, f32...) custom-call(f32[2,2048]{1,0:T(2,128)S(1)} %get-tuple-element.27.refs_0_, ...), custom_call_target="tpu_custom_call" | custom-call | tf_op jit(solution)/shard_map/exchange_0/pallas_call | solution.py:145
  26.3 0.0 copy-done.8
  26.3 0.0 copy-start.7
  26.3 27.1 %section_one.1 = (f32[2048,256]{1,0:T(8,128)S(1)}, f32[2048,256]{1,0:T(8,128)S(1)}, f32[2,2048]{1,0:T(2,128)S(1)}, f32[2,2048]{1,0:T(2,128)S(1)}, f32[2,64,256]{...) custom-call(f32[2048,256]{1,0:T(8,128)S(1)} %get-tuple-element.26.f.f0, ...), custom_call_target="tpu_custom_call" | custom-call | tf_op jit(solution)/shard_map/section_one/pallas_call | solution.py:418
  53.4 14.9 %exchange_1.1 = (f32[2,2048]{1,0:T(2,128)S(1)}, f32[2,2048]{1,0:T(2,128)S(1)}, f32[4,2,64,256]{3,2,1,0:T(8,128)S(1)}, f32[4,2,64,256]{3,2,1,0:T(8,128)S(1)}, f32[32,1,64]{2,1,0:T(1,128)S(1)}) custom-call(f32[2,2048]{1,0:T(2,128)S(1)} %get-tuple-element.39.refs_0_, f32[2,2048]{1,0:T(2,128)S(1)} %get-tuple-element.40.refs_1_, ...), custom_call_target="tpu_custom_call" | custom-call | tf_op jit(solution)/shard_map/exchange_1/pallas_call | solution.py:145
  68.3 0.0 copy-done.7
  68.3 9.6 %section_two.1 = (f32[64,32,256]{2,1,0:T(8,128)}, f32[1,32,64]{2,1,0:T(8,128)}) custom-call(f32[2048,256]{1,0:T(8,128)S(1)} %get-tuple-element.38.f, bf16[3,64,32,256]{3,2,1,0:T(8,128)(2,1)S(1)} %get-tuple-element.32.vel, f32[2,2048]{1,0:T(2,128)S(1)} %get-tuple-element.44.o_left, f32[2,2048]{1,0:T(2,128)S(1)} %get-tuple-element.45.o_right, ...), custom_call_target="tpu_custom_call" | custom-call | tf_op jit(solution)/shard_map/section_two/pallas_call | solution.py:447
  (2 shorter events, 0.0 us)
Async XLA Ops:
  0.6 1.6 %copy-start.1 = (f32[64,32,256]{2,1,0:T(8,128)S(1)}, f32[64,32,256]{2,1,0:T(8,128)}, u32[]{:S(2)}) copy-start(f32[64,32,256]{2,1,0:T(8,128)} %param.8) | copy-start | bytes 6291460
  2.2 0.7 copy-start.2
  2.9 0.7 copy-start.3
  3.7 0.7 copy-start.4
  4.4 0.7 copy-start.5
  5.1 0.7 copy-start.6
  8.4 17.9 %copy-start.8 = (s32[2]{0:T(128)S(1)}, s32[2]{0:T(128)}, u32[]{:S(2)}) copy-start(s32[2]{0:T(128)} %shear.3) | copy-start | bytes 28
  8.4 1.9 %copy-start = (bf16[3,64,32,256]{3,2,1,0:T(8,128)(2,1)S(1)}, bf16[3,64,32,256]{3,2,1,0:T(8,128)(2,1)}, u32[]{:S(2)}) copy-start(bf16[3,64,32,256]{3,2,1,0:T(8,128)(2,1)} %refs_5_.1) | copy-start | bytes 9437188
  26.3 42.0 %copy-start.7 = (s32[1,32]{1,0:T(1,128)S(1)}, s32[1,32]{1,0:T(1,128)}, u32[]{:S(2)}) copy-start(s32[1,32]{1,0:T(1,128)} %count.1) | copy-start | bytes 388
